TPU v7x, 256 devices: a whole 4x4x8 slice. The times are simulated.
256 devices in a mesh: gx: 4 (over x), gy: 8 (over y, core), gz: 8 (over z).
Axes of the slice: x: 4, y: 4, z: 8, core: 2. Of those that a mesh axis runs over, the one named last changes fastest.
Arguments:
- coarse_old: float32 [5, 64, 128, 4096], P(None, 'gx', 'gy', 'gz'), as said below
- fine_old: float32 [4096, 5, 4096], P(('gx', 'gy', 'gz'))
- slot_owner: int32 [4, 8, 256], P('gx', 'gy', 'gz'), may hold values from -1 to 31, as said below
- box_corner: int32 [4096, 3], P(('gx', 'gy', 'gz')), may hold values from 0 to 255, as said below
Outputs:
- coarse_new: float32 [5, 64, 128, 4096], P(None, 'gx', 'gy', 'gz')
- fine_new: float32 [4096, 5, 4096], P(('gx', 'gy', 'gz'))
Inputs may be any that keep to these rules, and one draw needn't show every extreme that they name: coarse_old and fine_old: density at least 1 and pressure at least 1 in every cell. `slot_owner`: an owner lies in the same gy index as the candidate. At most 2 refined candidates of one device have the same owner, and some device sends exactly 2 to one owner; every device owns exactly 16 fine boxes. `box_corner`: rows of one device are the 16 boxes it owns, each a candidate whose slot_owner names this device, ordered by the device that holds the candidate (gx slowest, then gz) and then by the candidate's coordinates (x slowest).
All inputs are finite; a program needn't handle non-finite values.
Results may differ from a plain program's by a relative error of at most 0.0003.
Values sent between devices are 32-bit elements; how exact they have to be, the bound alone decides.
A program may use at most 256 MiB of HBM per device.

v0:
```python
import jax
import jax.numpy as jnp
import numpy as np
from jax import lax
from jax.sharding import PartitionSpec as P

BOX = 16


HEAT_RATIO = 1.4
COURANT_NUMBER = 0.15


def extended(cells, sides, width):
    for axis, dim in sides:
        count = lax.axis_size(axis)
        head = lax.slice_in_dim(cells, 0, width, axis=dim)
        tail = lax.slice_in_dim(cells, cells.shape[dim] - width, cells.shape[dim], axis=dim)
        cells = jnp.concatenate(
            [
                lax.ppermute(tail, axis, [(i, (i + 1) % count) for i in range(count)]),
                cells,
                lax.ppermute(head, axis, [((i + 1) % count, i) for i in range(count)]),
            ],
            axis=dim,
        )
    return cells


def flux_speed(fields, direction):
    density = fields[0]
    momenta = [fields[1], fields[2], fields[3]]
    energy = fields[4]
    inverse = 1.0 / density
    velocity = [momenta[0] * inverse, momenta[1] * inverse, momenta[2] * inverse]
    kinetic = 0.5 * (momenta[0] * velocity[0] + momenta[1] * velocity[1] + momenta[2] * velocity[2])
    pressure = (HEAT_RATIO - 1.0) * (energy - kinetic)
    sound_speed = jnp.sqrt(HEAT_RATIO * pressure * inverse)
    normal_vel = velocity[direction]
    pieces = [momenta[direction]]
    for member in range(3):
        moment_flux = momenta[member] * normal_vel
        if member == direction:
            moment_flux = moment_flux + pressure
        pieces.append(moment_flux)
    pieces.append((energy + pressure) * normal_vel)
    return (jnp.stack(pieces), jnp.abs(normal_vel) + sound_speed)


def rusanov(lower_cells, upper_cells, direction):
    flux_lower, speed_lower = flux_speed(lower_cells, direction)
    flux_upper, speed_upper = flux_speed(upper_cells, direction)
    signal = jnp.maximum(speed_lower, speed_upper)
    return 0.5 * (flux_lower + flux_upper) - 0.5 * signal[None] * (upper_cells - lower_cells)


def wave_speed(fields):
    density = fields[0]
    inverse = 1.0 / density
    speed_x = fields[1] * inverse
    speed_y = fields[2] * inverse
    speed_z = fields[3] * inverse
    kinetic = 0.5 * (fields[1] * speed_x + fields[2] * speed_y + fields[3] * speed_z)
    pressure = (HEAT_RATIO - 1.0) * (fields[4] - kinetic)
    sound_speed = jnp.sqrt(HEAT_RATIO * pressure * inverse)
    return (
        jnp.maximum(jnp.maximum(jnp.abs(speed_x), jnp.abs(speed_y)), jnp.abs(speed_z)) + sound_speed
    )


def advance(padded, courant):
    interior = padded[..., 1:-1, 1:-1, 1:-1]
    flux_x = rusanov(padded[..., :-1, 1:-1, 1:-1], padded[..., 1:, 1:-1, 1:-1], 0)
    flux_y = rusanov(padded[..., 1:-1, :-1, 1:-1], padded[..., 1:-1, 1:, 1:-1], 1)
    flux_z = rusanov(padded[..., 1:-1, 1:-1, :-1], padded[..., 1:-1, 1:-1, 1:], 2)
    change = (
        flux_x[..., 1:, :, :]
        - flux_x[..., :-1, :, :]
        + (flux_y[..., :, 1:, :] - flux_y[..., :, :-1, :])
        + (flux_z[..., 1:] - flux_z[..., :-1])
    )
    return (interior - courant * change, (flux_x, flux_y, flux_z))


def zcut(piece, start_cut, stop_cut):
    length = piece.shape[-1]
    return piece.reshape(piece.shape[:-1] + (length // BOX, BOX))[..., start_cut:stop_cut]


def expand_z(piece, offset, extent_z):
    widths = [(0, 0)] * (piece.ndim - 1) + [(offset, BOX - offset - extent_z)]
    spread = jnp.pad(piece, widths)
    return spread.reshape(spread.shape[:-2] + (spread.shape[-2] * BOX,))


def coarse_faces(coarse):
    core = BOX // 2
    shift = BOX // 4
    size_x, size_y, size_z = (coarse.shape[1], coarse.shape[2], coarse.shape[3])
    blocked = coarse.reshape(5, size_x // BOX, BOX, size_y // BOX, BOX, size_z)
    boundary = []
    for first_cell in (shift - 1, shift + core - 1):
        lower_cells = zcut(
            blocked[:, :, first_cell, :, shift : shift + core, :], shift, shift + core
        )
        upper_cells = zcut(
            blocked[:, :, first_cell + 1, :, shift : shift + core, :], shift, shift + core
        )
        boundary.append(rusanov(lower_cells, upper_cells, 0).transpose(1, 2, 4, 0, 3, 5))
    for first_cell in (shift - 1, shift + core - 1):
        lower_cells = zcut(
            blocked[:, :, shift : shift + core, :, first_cell, :], shift, shift + core
        )
        upper_cells = zcut(
            blocked[:, :, shift : shift + core, :, first_cell + 1, :], shift, shift + core
        )
        boundary.append(rusanov(lower_cells, upper_cells, 1).transpose(1, 3, 4, 0, 2, 5))
    for first_cell in (shift - 1, shift + core - 1):
        inner = blocked[:, :, shift : shift + core, :, shift : shift + core, :]
        lower_cells = zcut(inner, first_cell, first_cell + 1)[..., 0]
        upper_cells = zcut(inner, first_cell + 1, first_cell + 2)[..., 0]
        boundary.append(rusanov(lower_cells, upper_cells, 2).transpose(1, 3, 5, 0, 2, 4))
    stacked = jnp.stack(boundary, axis=4)
    return stacked.reshape(stacked.shape[:4] + (6 * core * core,))


def apply_fine(advanced, coarse_flux, register, average, refined, courant):
    core = BOX // 2
    shift = BOX // 4
    size_x, size_y, size_z = (advanced.shape[1], advanced.shape[2], advanced.shape[3])
    blocks_x, blocks_y, blocks_z = (size_x // BOX, size_y // BOX, size_z // BOX)
    blocked = advanced.reshape(5, blocks_x, BOX, blocks_y, BOX, size_z)
    mismatch = jnp.where(refined[:, :, :, None, None], courant * (coarse_flux - register), 0.0)
    mismatch = mismatch.reshape(blocks_x, blocks_y, blocks_z, 5, 6, core, core)
    lower_x = expand_z(mismatch[:, :, :, :, 0].transpose(3, 0, 1, 4, 2, 5), shift, core)
    upper_x = expand_z(mismatch[:, :, :, :, 1].transpose(3, 0, 1, 4, 2, 5), shift, core)
    blocked = blocked.at[:, :, shift - 1, :, shift : shift + core, :].add(lower_x)
    blocked = blocked.at[:, :, shift + core, :, shift : shift + core, :].add(-upper_x)
    lower_y = expand_z(mismatch[:, :, :, :, 2].transpose(3, 0, 4, 1, 2, 5), shift, core)
    upper_y = expand_z(mismatch[:, :, :, :, 3].transpose(3, 0, 4, 1, 2, 5), shift, core)
    blocked = blocked.at[:, :, shift : shift + core, :, shift - 1, :].add(lower_y)
    blocked = blocked.at[:, :, shift : shift + core, :, shift + core, :].add(-upper_y)
    lower_z = expand_z(mismatch[:, :, :, :, 4].transpose(3, 0, 4, 1, 5, 2)[..., None], shift - 1, 1)
    upper_z = expand_z(
        mismatch[:, :, :, :, 5].transpose(3, 0, 4, 1, 5, 2)[..., None], shift + core, 1
    )
    region = blocked[:, :, shift : shift + core, :, shift : shift + core, :]
    region = region + lower_z - upper_z
    marks = jnp.broadcast_to(
        refined.astype(jnp.float32)[None, :, None, :, None, :, None],
        (1, blocks_x, core, blocks_y, core, blocks_z, core),
    )
    inside = expand_z(marks, shift, core) > 0.5
    filling = expand_z(
        average.reshape(blocks_x, blocks_y, blocks_z, 5, core, core, core).transpose(
            3, 0, 4, 1, 5, 2, 6
        ),
        shift,
        core,
    )
    region = jnp.where(inside, filling, region)
    blocked = blocked.at[:, :, shift : shift + core, :, shift : shift + core, :].set(region)
    return blocked.reshape(5, size_x, size_y, size_z)


def flat_tables():
    core = BOX // 2
    edge = BOX + 2
    rows_y, cols_z = np.meshgrid(np.arange(edge), np.arange(edge), indexing="ij")
    rows_y = rows_y.reshape(-1)
    cols_z = cols_z.reshape(-1)
    inside_yz = (rows_y >= 1) & (rows_y <= BOX) & (cols_z >= 1) & (cols_z <= BOX)
    fill_index = np.where(inside_yz, (rows_y - 1) * BOX + (cols_z - 1), 0).astype(np.int32)
    ghost_yz = ((rows_y + 1) // 2 * (core + 2) + (cols_z + 1) // 2).astype(np.int32)
    ghost_x = ((np.arange(edge) + 1) // 2).astype(np.int32)
    plane_x = (np.arange(edge) >= 1) & (np.arange(edge) <= BOX)
    inner_mask = plane_x[:, None] & inside_yz[None, :]
    inner_y, inner_z = np.meshgrid(np.arange(1, BOX + 1), np.arange(1, BOX + 1), indexing="ij")
    inner_index = (inner_y * edge + inner_z).reshape(-1).astype(np.int32)
    return (fill_index, ghost_yz, ghost_x, inner_mask, inner_index)


def fine_step(fine_rows, old_rows, new_rows, courant):
    core = BOX // 2
    edge = BOX + 2
    flat = edge * edge
    count = fine_rows.shape[0]
    fill_index, ghost_yz, ghost_x, inner_mask, inner_index = flat_tables()
    side = np.arange(1, BOX + 1).astype(np.int32)
    fine_state = fine_rows.transpose(1, 0, 2).reshape(5, count, BOX, BOX * BOX)
    fine_state = jnp.pad(fine_state, ((0, 0), (0, 0), (1, 1), (0, 0)))
    fine_state = jnp.take(fine_state, jnp.asarray(fill_index), axis=3)
    patch_old = old_rows.transpose(1, 0, 2).reshape(5, count, core + 2, (core + 2) ** 2)
    patch_new = new_rows.transpose(1, 0, 2).reshape(5, count, core + 2, (core + 2) ** 2)
    mask_cells = jnp.asarray(inner_mask)
    summed = None
    region = None
    for substep in range(2):
        if substep == 0:
            coarse_now = patch_old
        else:
            coarse_now = 0.5 * (patch_old + patch_new)
        ghost_cells = jnp.take(
            jnp.take(coarse_now, jnp.asarray(ghost_x), axis=2), jnp.asarray(ghost_yz), axis=3
        )
        padded = jnp.where(mask_cells, fine_state, ghost_cells)
        flux_x = rusanov(padded[:, :, :-1], padded[:, :, 1:], 0)
        flux_y = rusanov(padded[..., :-edge], padded[..., edge:], 1)
        flux_z = rusanov(padded[..., :-1], padded[..., 1:], 2)
        interior = padded[:, :, 1 : edge - 1, edge : flat - edge]
        change = (
            flux_x[:, :, 1 : edge - 1, edge : flat - edge]
            - flux_x[:, :, 0 : edge - 2, edge : flat - edge]
            + (
                flux_y[:, :, 1 : edge - 1, edge : flat - edge]
                - flux_y[:, :, 1 : edge - 1, 0 : flat - 2 * edge]
            )
            + (
                flux_z[:, :, 1 : edge - 1, edge : flat - edge]
                - flux_z[:, :, 1 : edge - 1, edge - 1 : flat - edge - 1]
            )
        )
        region = interior - courant * change
        face_lists = [
            jnp.take(flux_x[:, :, 0], jnp.asarray(inner_index), axis=2),
            jnp.take(flux_x[:, :, BOX], jnp.asarray(inner_index), axis=2),
            jnp.take(flux_y[:, :, 1 : BOX + 1], jnp.asarray(side), axis=3),
            jnp.take(flux_y[:, :, 1 : BOX + 1], jnp.asarray(BOX * edge + side), axis=3),
            jnp.take(flux_z[:, :, 1 : BOX + 1], jnp.asarray(side * edge), axis=3),
            jnp.take(flux_z[:, :, 1 : BOX + 1], jnp.asarray(side * edge + BOX), axis=3),
        ]
        boundary = jnp.stack([piece.reshape(5, count, BOX, BOX) for piece in face_lists], axis=2)
        coarse_face = boundary.reshape(5, count, 6, core, 2, core, 2).sum(axis=(4, 6)) * 0.25
        summed = coarse_face if summed is None else summed + coarse_face
        fine_state = jnp.pad(region, ((0, 0), (0, 0), (1, 1), (edge, edge)))
    register = 0.5 * summed
    fine_done = jnp.take(region, jnp.asarray(inner_index - edge), axis=3)
    average = fine_done.reshape(5, count, core, 2, core, 2, core, 2).sum(axis=(3, 5, 7)) * 0.125
    return (fine_done.reshape(5, count, BOX**3).transpose(1, 0, 2), register, average)


def pack_results(register, average):
    core = BOX // 2
    count = register.shape[1]
    joined = jnp.concatenate(
        [average.reshape(5, count, core**3), register.reshape(5, count, 6 * core * core)], axis=2
    )
    return joined.transpose(1, 0, 2)


def candidate_patches(coarse):
    core = BOX // 2
    shift = BOX // 4
    size_x, size_y, size_z = (coarse.shape[1], coarse.shape[2], coarse.shape[3])
    blocks_x, blocks_y, blocks_z = (size_x // BOX, size_y // BOX, size_z // BOX)
    blocked = coarse.reshape(5, blocks_x, BOX, blocks_y, BOX, size_z)[
        :, :, shift - 1 : shift + core + 1, :, shift - 1 : shift + core + 1, :
    ]
    window = blocked.reshape(5, blocks_x, core + 2, blocks_y, core + 2, blocks_z, BOX)[
        ..., shift - 1 : shift + core + 1
    ]
    return window.transpose(1, 3, 5, 0, 2, 4, 6).reshape(
        blocks_x * blocks_y * blocks_z, 5, (core + 2) ** 3
    )


def across(buffer):
    return lax.all_to_all(buffer, ("gx", "gz"), split_axis=0, concat_axis=0, tiled=True)


def local(coarse_old, fine_old, slot_owner, box_corner):
    core = BOX // 2
    volume = core**3
    packed_len = volume + 6 * core * core
    owned_boxes = fine_old.shape[0]
    count_gx = lax.axis_size("gx")
    count_gz = lax.axis_size("gz")
    peer_count = count_gx * count_gz
    capacity = max(2, 2 * owned_boxes // peer_count)
    lane_count = peer_count * capacity
    extent = slot_owner.shape
    slot_count = extent[0] * extent[1] * extent[2]
    local_top = jnp.maximum(
        jnp.max(wave_speed(coarse_old)), jnp.max(wave_speed(fine_old.transpose(1, 0, 2)))
    )
    fastest = lax.pmax(local_top, ("gx", "gy", "gz"))
    courant = COURANT_NUMBER / fastest
    padded = extended(coarse_old, (("gx", 1), ("gy", 2), ("gz", 3)), 1)
    advanced = advance(padded, courant)[0]
    coarse_flux = coarse_faces(coarse_old)
    patch_old = candidate_patches(coarse_old)
    patch_new = candidate_patches(advanced)
    owners = slot_owner.reshape(slot_count)
    slot_index = jnp.arange(slot_count, dtype=jnp.int32)
    send_rank = jnp.sum(
        (owners[:, None] == owners[None, :]) & (slot_index[None, :] < slot_index[:, None]), axis=1
    )
    lane_ids = jnp.arange(lane_count, dtype=jnp.int32)
    matches = (owners[None, :] == (lane_ids // capacity)[:, None]) & (
        send_rank[None, :] == (lane_ids % capacity)[:, None]
    )
    picked = jnp.sum(jnp.where(matches, slot_index[None, :], 0), axis=1)
    slot_lane = jnp.where(owners >= 0, owners * capacity + send_rank, 0)
    source = box_corner[:, 0] // extent[0] * count_gz + box_corner[:, 2] // extent[2]
    box_index = jnp.arange(owned_boxes, dtype=jnp.int32)
    recv_rank = jnp.sum(
        (source[:, None] == source[None, :]) & (box_index[None, :] < box_index[:, None]), axis=1
    )
    box_lane = source * capacity + recv_rank
    outgoing = jnp.concatenate([patch_old, patch_new], axis=1)[picked]
    arrived = across(outgoing)[box_lane]
    fine_out, register, average = fine_step(fine_old, arrived[:, :5], arrived[:, 5:], courant)
    packed = pack_results(register, average)
    returning = jnp.zeros((lane_count, 5, packed_len), jnp.float32).at[box_lane].set(packed)
    per_slot = across(returning)[slot_lane]
    slot_table = per_slot.reshape(tuple(extent) + (5, packed_len))
    coarse_new = apply_fine(
        advanced,
        coarse_flux,
        slot_table[..., volume:],
        slot_table[..., :volume],
        slot_owner >= 0,
        courant,
    )
    return (coarse_new, fine_out)


def solution(mesh):
    in_specs = (
        P(None, "gx", "gy", "gz"),
        P(("gx", "gy", "gz"), None, None),
        P("gx", "gy", "gz"),
        P(("gx", "gy", "gz"), None),
    )
    out_specs = (P(None, "gx", "gy", "gz"), P(("gx", "gy", "gz"), None, None))
    return jax.shard_map(local, mesh=mesh, in_specs=in_specs, out_specs=out_specs, check_vma=False)
```

profile of v0, /device:TPU:4, one launch (start us, length us, event | category | flops | bytes accessed | tf_op | source)
XLA Modules:
  0.0 850.8 jit_solution(8082630658794050263)
XLA Ops:
  16.0 18.1 %slice_reduce_fusion = (f32[8,8,32]{2,1,0:T(8,128)}, f32[8,8,32]{2,1,0:T(8,128)S(1)}, f32[8,8,32]{2,1,0:T(8,128)S(1)}, f32[8,8,32]{2,1,0:T(8,128)S(1)}, f32[8,8,...) fusion(f32[5,1,8,1,8,32,16]{6,5,4,2,0,3,1:T(8,128)} %reshape.3872), kind=kLoop, calls=%fused_computation.113 | loop fusion | flops 8192 | bytes 311296 | tf_op jit(solution)/shard_map/slice | solution.py:33
  70.8 8.9 %slice_bitcast_fusion.1 = f32[1,1,32,5,10,10,10]{6,2,1,5,4,3,0:T(8,128)} fusion(f32[5,1,10,1,10,32,16]{6,5,3,4,2,0,1:T(8,128)} %reshape.3875), kind=kLoop, calls=%fused_computation.33 | loop fusion | bytes 1280000 | tf_op jit(solution)/shard_map/transpose | solution.py:262
  92.6 78.4 %pmax.7 = f32[]{:T(128)} all-reduce(f32[]{:T(128)S(6)} %max.105), channel_id=1, replica_groups=mesh['gx'=4,'gy'=8,'gz'=8] {'gx','gy','gz'}, use_global_device_ids=true, to_apply=%region_2.0 | all-reduce | flops 1 | bytes 8 | tf_op jit(solution)/shard_map/pmax | solution.py:286
  181.2 7.4 copy.5396
  201.4 19.3 %gather_fusion = f32[324,5,16,16]{3,2,1,0:T(8,128)} fusion(f32[5,16,16,256]{2,1,3,0:T(8,128)} %copy.5394, s32[1024]{0:T(1024)S(1)} %pad_clamp_fusion.11), kind=kCustom, calls=%fused_computation.16 | custom fusion | bytes 3319056 | tf_op jit(solution)/shard_map/jit(_take)/gather | solution.py:192
  220.7 10.4 %copy.5395 = f32[324,5,16,16]{0,2,3,1:T(8,128)} copy(f32[324,5,16,16]{3,2,1,0:T(8,128)} %gather_fusion) | data formatting | bytes 3317760 | tf_op jit(solution)/shard_map/jit(_take)/gather | solution.py:192
  288.3 8.9 %slice_bitcast_fusion = f32[1,1,32,5,10,10,10]{6,2,1,5,4,3,0:T(8,128)} fusion(f32[5,1,10,1,10,32,16]{6,5,3,4,2,0,1:T(8,128)} %reshape.3877), kind=kLoop, calls=%fused_computation.32 | loop fusion | bytes 1280000 | tf_op jit(solution)/shard_map/transpose | solution.py:262
  297.1 7.4 copy.5398
  344.9 71.7 %all-to-all-done = f32[64,10,1000]{2,1,0:T(8,128)} async-done(((f32[64,10,1000]{2,1,0:T(8,128)}), f32[64,10,1000]{2,1,0:T(8,128)}, u32[]{:S(2)}, u32[]{:S(2)}) %all-to-all-start) | async-done | bytes 2560032 | tf_op jit(solution)/shard_map/all_to_all | solution.py:268
  424.0 17.5 %gather_fusion.6 = f32[324,5,16,18]{3,2,1,0:T(8,128)} fusion(f32[5,16,18,100]{2,1,3,0:T(8,128)} %copy.5403, s32[1024]{0:T(1024)S(1)} %get-tuple-element.344), kind=kCustom, calls=%fused_computation.1.clone | custom fusion | bytes 3733776 | tf_op jit(solution)/shard_map/jit(_take)/gather | solution.py:203
  441.4 9.8 %copy.5404 = f32[324,5,16,18]{0,2,3,1:T(8,128)S(1)} copy(f32[324,5,16,18]{3,2,1,0:T(8,128)} %gather_fusion.6) | data formatting | bytes 3732480 | tf_op jit(solution)/shard_map/jit(_take)/gather | solution.py:203
  471.2 17.6 %gather_fusion.8 = f32[324,5,16,18]{3,2,1,0:T(8,128)} fusion(f32[5,16,18,100]{2,1,3,0:T(8,128)} %copy.5408, s32[1024]{0:T(1024)S(1)} %get-tuple-element.344), kind=kCustom, calls=%fused_computation.6.clone | custom fusion | bytes 3733776 | tf_op jit(solution)/shard_map/jit(_take)/gather | solution.py:203
  488.9 10.4 %copy.5409 = f32[324,5,16,18]{0,2,3,1:T(8,128)} copy(f32[324,5,16,18]{3,2,1,0:T(8,128)} %gather_fusion.8) | data formatting | bytes 3732480 | tf_op jit(solution)/shard_map/jit(_take)/gather | solution.py:203
  505.7 9.5 %copy.5416 = f32[5,16,16,306]{2,1,3,0:T(8,128)} copy(f32[5,16,16,306]{3,1,2,0:T(8,128)} %slice.1649) | data formatting | bytes 3133440 | tf_op jit(solution)/shard_map/slice | solution.py:227
  538.2 9.5 %copy.5428 = f32[5,16,16,306]{2,1,3,0:T(8,128)} copy(f32[5,16,16,306]{3,1,2,0:T(8,128)} %slice.1653) | data formatting | bytes 3133440 | tf_op jit(solution)/shard_map/slice | solution.py:227
  561.9 9.8 %copy.5420 = f32[5,16,16,323]{2,1,3,0:T(8,128)} copy(f32[5,16,16,323]{3,1,2,0:T(8,128)} %slice.1650) | data formatting | bytes 3307520 | tf_op jit(solution)/shard_map/slice | solution.py:229
  593.7 10.2 %copy.5432 = f32[5,16,16,323]{2,1,3,0:T(8,128)} copy(f32[5,16,16,323]{3,1,2,0:T(8,128)} %slice.1654) | data formatting | bytes 3307520 | tf_op jit(solution)/shard_map/slice | solution.py:229
  676.5 8.2 copy.5410
  684.7 9.6 %gather_fusion.3 = f32[256,5,16,16]{3,2,1,0:T(8,128)} fusion(f32[5,16,16,288]{2,1,3,0:T(8,128)} %copy.5410, s32[1024]{0:T(1024)} %get-tuple-element.343), kind=kCustom, calls=%fused_computation.19 | custom fusion | bytes 2622464 | tf_op jit(solution)/shard_map/jit(_take)/gather | solution.py:237
  694.3 12.7 %copy.5411 = f32[5,16,16,256]{1,3,2,0:T(8,128)} copy(f32[5,16,16,256]{2,1,0,3:T(8,128)} %bitcast.755) | data formatting | bytes 2621440 | tf_op jit(solution)/shard_map/jit(_take)/gather | solution.py:237
  707.0 10.5 %reduce_sum.65 = f32[5,16,8,8,8]{1,4,3,2,0:T(8,128)S(1)} reduce(f32[5,16,8,2,8,2,8,2]{1,7,6,5,4,3,2,0:T(2,128)} %bitcast.757, f32[]{:T(128)} %constant.420.clone.1), dimensions={3,5,7}, to_apply=%region_6.9 | reduce | flops 286720 | bytes 1474564 | tf_op jit(solution)/shard_map/reduce_sum | solution.py:238
  722.2 8.5 all-to-all-start.1
  740.6 12.6 %fusion = (f32[5,8,8,32]{3,2,1,0:T(8,128)S(1)}, f32[5,8,8,32]{3,2,1,0:T(8,128)S(1)}) fusion(f32[5,1,8,1,8,32,16]{6,5,4,2,0,3,1:T(8,128)} %reshape.3872), kind=kLoop, calls=%fused_computation.45 | loop fusion | flops 20480 | bytes 245760 | tf_op jit(solution)/shard_map/sub | solution.py:54
  765.4 7.6 all-to-all-done.1
  (814 shorter events, 451.0 us)
Async XLA Ops:
  2.5 230.0 %collective-permute-start = (f32[5,1,16,512]{3,2,0,1:T(8,128)}, f32[5,1,16,512]{3,2,0,1:T(8,128)}, u32[]{:S(2)}, u32[]{:S(2)}) collective-permute-start(f32[5,1,16,512]{3,2,0,1:T(8,128)} %copy.5535), channel_id=1, source_target_pairs={{0,64},{64,128},{128,192},{192,0},{1,65},{65,129},{129,193},{193,1... | collective-permute-start | bytes 491528 | tf_op jit(solution)/shard_map/ppermute | solution.py:21
  4.4 231.9 %collective-permute-start.1 = (f32[5,1,16,512]{3,2,0,1:T(8,128)}, f32[5,1,16,512]{3,2,0,1:T(8,128)}, u32[]{:S(2)}, u32[]{:S(2)}) collective-permute-start(f32[5,1,16,512]{3,2,0,1:T(8,128)} %copy.5536), channel_id=1, source_target_pairs={{64,0},{128,64},{192,128},{0,192},{65,1},{129,65},{193,129},{1,193... | collective-permute-start | bytes 491528 | tf_op jit(solution)/shard_map/ppermute | solution.py:23
  34.1 48.4 %copy-start.60 = (f32[8,8,32]{2,1,0:T(8,128)}, f32[8,8,32]{2,1,0:T(8,128)S(1)}, u32[]{:S(2)}) copy-start(f32[8,8,32]{2,1,0:T(8,128)S(1)} %get-tuple-element.134) | copy-start | bytes 24580
  34.1 49.0 %copy-start.90 = (f32[8,8,32]{2,1,0:T(8,128)}, f32[8,8,32]{2,1,0:T(8,128)S(1)}, u32[]{:S(2)}) copy-start(f32[8,8,32]{2,1,0:T(8,128)S(1)} %get-tuple-element.130) | copy-start | bytes 24580
  34.1 49.6 %copy-start.88 = (f32[8,8,32]{2,1,0:T(8,128)}, f32[8,8,32]{2,1,0:T(8,128)S(1)}, u32[]{:S(2)}) copy-start(f32[8,8,32]{2,1,0:T(8,128)S(1)} %get-tuple-element.128) | copy-start | bytes 24580
  34.1 50.2 %copy-start.86 = (f32[8,8,32]{2,1,0:T(8,128)}, f32[8,8,32]{2,1,0:T(8,128)S(1)}, u32[]{:S(2)}) copy-start(f32[8,8,32]{2,1,0:T(8,128)S(1)} %get-tuple-element.125) | copy-start | bytes 24580
  34.1 50.8 %copy-start.84 = (f32[8,8,32]{2,1,0:T(8,128)}, f32[8,8,32]{2,1,0:T(8,128)S(1)}, u32[]{:S(2)}) copy-start(f32[8,8,32]{2,1,0:T(8,128)S(1)} %get-tuple-element.123) | copy-start | bytes 24580
  34.1 51.4 %copy-start.82 = (f32[8,8,32]{2,1,0:T(8,128)}, f32[8,8,32]{2,1,0:T(8,128)S(1)}, u32[]{:S(2)}) copy-start(f32[8,8,32]{2,1,0:T(8,128)S(1)} %get-tuple-element.120) | copy-start | bytes 24580
  34.1 51.4 %copy-start.80 = (f32[8,8,32]{2,1,0:T(8,128)}, f32[8,8,32]{2,1,0:T(8,128)S(1)}, u32[]{:S(2)}) copy-start(f32[8,8,32]{2,1,0:T(8,128)S(1)} %get-tuple-element.118) | copy-start | bytes 24580
  44.1 44.3 %copy-start.76 = (f32[1,1,8,1,32,8]{4,5,3,2,1,0:T(8,128)}, f32[1,1,8,1,32,8]{4,5,3,2,1,0:T(8,128)S(1)}, u32[]{:S(2)}) copy-start(f32[1,1,8,1,32,8]{4,5,3,2,1,0:T(8,128)S(1)} %copy.5503) | copy-start | bytes 24580
  45.1 41.8 %copy-start.78 = (f32[1,1,8,1,32,8]{4,5,3,2,1,0:T(8,128)}, f32[1,1,8,1,32,8]{4,5,3,2,1,0:T(8,128)S(1)}, u32[]{:S(2)}) copy-start(f32[1,1,8,1,32,8]{4,5,3,2,1,0:T(8,128)S(1)} %copy.5498) | copy-start | bytes 24580
  52.9 38.3 %copy-start.62 = (f32[1,1,8,1,32,8]{4,5,3,2,1,0:T(8,128)}, f32[1,1,8,1,32,8]{4,5,3,2,1,0:T(8,128)S(1)}, u32[]{:S(2)}) copy-start(f32[1,1,8,1,32,8]{4,5,3,2,1,0:T(8,128)S(1)} %copy.5515) | copy-start | bytes 24580
  54.9 34.9 %copy-start.65 = (f32[1,1,8,1,32,8]{4,5,3,2,1,0:T(8,128)}, f32[1,1,8,1,32,8]{4,5,3,2,1,0:T(8,128)S(1)}, u32[]{:S(2)}) copy-start(f32[1,1,8,1,32,8]{4,5,3,2,1,0:T(8,128)S(1)} %copy.5510) | copy-start | bytes 24580
  70.8 21.8 %copy-start.198 = (s32[324]{0:T(512)S(1)}, s32[324]{0:T(512)}, u32[]{:S(2)}) copy-start(s32[324]{0:T(512)} %constant.617) | copy-start | bytes 3892
  70.8 100.2 %copy-start.24 = (f32[5,1,1,8,32,16]{5,4,3,0,2,1:T(8,128)S(1)}, f32[5,1,1,8,32,16]{5,4,3,0,2,1:T(8,128)}, u32[]{:S(2)}) copy-start(f32[5,1,1,8,32,16]{5,4,3,0,2,1:T(8,128)} %copy-done.23) | copy-start | bytes 245764
  79.7 91.5 %copy-start.26 = (f32[5,1,1,8,32,16]{5,4,3,0,2,1:T(8,128)S(1)}, f32[5,1,1,8,32,16]{5,4,3,0,2,1:T(8,128)}, u32[]{:S(2)}) copy-start(f32[5,1,1,8,32,16]{5,4,3,0,2,1:T(8,128)} %copy-done.25) | copy-start | bytes 245764
  79.7 91.7 %copy-start.28 = (f32[5,1,1,8,32,16]{5,4,3,0,2,1:T(8,128)S(1)}, f32[5,1,1,8,32,16]{5,4,3,0,2,1:T(8,128)}, u32[]{:S(2)}) copy-start(f32[5,1,1,8,32,16]{5,4,3,0,2,1:T(8,128)} %copy-done.27) | copy-start | bytes 245764
  86.9 84.8 %copy-start.30 = (f32[5,1,1,8,32,16]{5,4,3,0,2,1:T(8,128)S(1)}, f32[5,1,1,8,32,16]{5,4,3,0,2,1:T(8,128)}, u32[]{:S(2)}) copy-start(f32[5,1,1,8,32,16]{5,4,3,0,2,1:T(8,128)} %copy-done.29) | copy-start | bytes 245764
  237.6 6.4 collective-permute-start.3
  238.1 6.2 collective-permute-start.2
  248.8 13.7 %collective-permute-start.4 = (f32[5,18,18,1]{2,3,1,0:T(1,128)}, f32[5,18,18,1]{2,3,1,0:T(1,128)}, u32[]{:S(2)}, u32[]{:S(2)}) collective-permute-start(f32[5,18,18,1]{2,3,1,0:T(1,128)} %copy.5333), channel_id=1, source_target_pairs={{0,1},{1,2},{2,3},{3,4},{4,5},{5,6},{6,7},{7,0},{8,9},{9,10},{10,1... | collective-permute-start | bytes 19448 | tf_op jit(solution)/shard_map/ppermute | solution.py:21
  252.3 12.7 %collective-permute-start.5 = (f32[5,18,18,1]{2,3,1,0:T(1,128)}, f32[5,18,18,1]{2,3,1,0:T(1,128)}, u32[]{:S(2)}, u32[]{:S(2)}) collective-permute-start(f32[5,18,18,1]{2,3,1,0:T(1,128)} %copy.5335), channel_id=1, source_target_pairs={{1,0},{2,1},{3,2},{4,3},{5,4},{6,5},{7,6},{0,7},{9,8},{10,9},{11,1... | collective-permute-start | bytes 19448 | tf_op jit(solution)/shard_map/ppermute | solution.py:23
  315.1 101.4 %all-to-all-start = ((f32[64,10,1000]{2,1,0:T(8,128)}), f32[64,10,1000]{2,1,0:T(8,128)}, u32[]{:S(2)}, u32[]{:S(2)}) async-start(f32[64,10,1000]{2,1,0:T(8,128)} %gather_fusion.1), calls=%async_computation | async-start | bytes 8388608 | tf_op jit(solution)/shard_map/all_to_all | solution.py:268
  722.2 50.7 %all-to-all-start.1 = ((f32[64,5,896]{2,1,0:T(8,128)}), f32[64,5,896]{2,1,0:T(8,128)S(1)}, u32[]{:S(2)}, u32[]{:S(2)}) async-start(f32[64,5,896]{2,1,0:T(8,128)} %scatter_fusion), calls=%async_computation.1 | async-start | bytes 3670016 | tf_op jit(solution)/shard_map/all_to_all | solution.py:268
  (196 other events, 1469.7 us)
where the time goes:
time: 860 us; the launch traced here: 851 us
  local copies, waits for them, and re-layouts  490 us (57%)
  other arithmetic  175 us (20%)
  waiting for transfers between devices  79.5 us (9%)
  blocking collectives  78.4 us (9%)
  starting transfers between devices  21.7 us (3%)
    all_to_all x2, waiting for transfers between devices, across(): lax.all_to_all(buffer, ('gx', 'gz'), split_axis=0, concat_axis=0, tiled=T...  79.2 us
    pmax x1, blocking collectives, local(): fastest = lax.pmax(local_top, ('gx', 'gy', 'gz'))  78.4 us
    unnamed x508, local copies, waits for them, and re-layouts  72.6 us
    gather x4, local copies, waits for them, and re-layouts, fine_step(): jnp.take(jnp.take(coarse_now, jnp.asarray(ghost_x), axis=2), jnp.asarray(...  55.3 us
    unnamed x84, other arithmetic  43.3 us
    transpose x4, local copies, waits for them, and re-layouts, candidate_patches(): window.transpose(1, 3, 5, 0, 2, 4, 6)  32.5 us
    gather x2, local copies, waits for them, and re-layouts, fine_step(): fine_state = jnp.take(fine_state, jnp.asarray(fill_index), axis=3)  29.7 us
    gather x4, local copies, waits for them, and re-layouts, fine_step(): fine_done = jnp.take(region, jnp.asarray(inner_index - edge), axis=3)  29.4 us
  transfers between devices with their start and end apart: 8, of which 3 were waited for; matrix products, arithmetic and copies ran while one was open for 26% of the time, Pallas kernels for 0%

commit v1 on v0

v1 whole, which is shorter than its diff:
```python
import functools

import jax
import jax.numpy as jnp
import numpy as np
from jax import lax
from jax.experimental import pallas as pl
from jax.experimental.pallas import tpu as pltpu
from jax.sharding import PartitionSpec as P

BOX = 16
CORE = 8
SHIFT = 4
HEAT_RATIO = 1.4
COURANT_NUMBER = 0.15
OUT_ROWS = 32
BACK_ROWS = 40
MESH = pl.DeviceIdType.MESH
F32 = jnp.float32
BF16 = jnp.bfloat16
VMEM_LIMIT = 56 * 1024 * 1024


def speeds(u):
    inverse = 1.0 / u[0]
    velocity = [u[1] * inverse, u[2] * inverse, u[3] * inverse]
    kinetic = 0.5 * (u[1] * velocity[0] + u[2] * velocity[1] + u[3] * velocity[2])
    pressure = (HEAT_RATIO - 1.0) * (u[4] - kinetic)
    sound = jnp.sqrt(HEAT_RATIO * pressure * inverse)
    return velocity, pressure, sound


def dirflux(u, prims, d):
    velocity, pressure, sound = prims
    normal = velocity[d]
    flux = [u[1 + d]]
    for m in range(3):
        piece = u[1 + m] * normal
        flux.append(piece + pressure if m == d else piece)
    flux.append((u[4] + pressure) * normal)
    return flux, jnp.abs(normal) + sound


def face(ul, fl, sl, ur, fr, sr):
    half = 0.5 * jnp.maximum(sl, sr)
    return [0.5 * (a + b) - half * (d - c) for a, b, c, d in zip(fl, fr, ul, ur)]


def fastest_of(prims):
    velocity, _, sound = prims
    top = jnp.maximum(jnp.abs(velocity[0]), jnp.abs(velocity[1]))
    return jnp.maximum(top, jnp.abs(velocity[2])) + sound


def fold(top):
    best = None
    for row in range(0, top.shape[0], 8):
        for lane in range(0, top.shape[1], 128):
            tile = top[row : row + 8, lane : lane + 128]
            best = tile if best is None else jnp.maximum(best, tile)
    return best


def split3(x):
    high = x.astype(BF16)
    rest = x - high.astype(F32)
    middle = rest.astype(BF16)
    low = (rest - middle.astype(F32)).astype(BF16)
    return high, middle, low


def put_split(ref, row, count, x):
    for part, piece in enumerate(split3(x)):
        ref[pl.ds(part * count + row, x.shape[0]), :] = piece


def sum_split(product):
    count = product.shape[0] // 3
    return product[:count] + product[count : 2 * count] + product[2 * count :]


def dot_nt(a, b):
    return lax.dot_general(a, b, (((1,), (1,)), ((), ())), preferred_element_type=F32)


def dot_nn(a, b):
    return lax.dot_general(a, b, (((1,), (0,)), ((), ())), preferred_element_type=F32)


def onehot(key_row, rows):
    index = lax.broadcasted_iota(jnp.int32, (rows, key_row.shape[1]), 0)
    return jnp.where(index == key_row, 1.0, 0.0).astype(BF16)


def coarse_kernel(coarse, keys, fine, pay, chgl, hy, hz, finet, top, chgf, pflux, pspeed, cxy, cz, rxy):
    nx, ny, nz = coarse.shape[1:]
    row = lax.broadcasted_iota(jnp.int32, (ny, nz), 0)
    lane = lax.broadcasted_iota(jnp.int32, (ny, nz), 1)
    spot = lane % BOX
    refined = jnp.broadcast_to(keys[2:3, :], (ny, nz)) >= 0
    row_in = (row >= SHIFT) & (row < SHIFT + CORE)
    lane_in = refined & (spot >= SHIFT) & (spot < SHIFT + CORE)

    def mark(mask):
        return jnp.where(mask, 1.0, 0.0)

    at_x = mark(row_in & lane_in)
    at_y_lo = mark(lane_in & ((row == SHIFT) | (row == SHIFT + CORE)))
    at_y_hi = mark(lane_in & ((row == SHIFT - 1) | (row == SHIFT + CORE - 1)))
    at_z_lo = mark(refined & row_in & ((spot == SHIFT) | (spot == SHIFT + CORE)))
    at_z_hi = mark(refined & row_in & ((spot == SHIFT - 1) | (spot == SHIFT + CORE - 1)))
    keep_row = mark(row > 0)
    keep_lane = mark(lane > 0)
    lane_tile = lax.broadcasted_iota(jnp.int32, (ny, 128), 1)

    def plane(x, best):
        before = jnp.maximum(x - 1, 0)
        u = [coarse[f, x] for f in range(5)]
        prims = speeds(u)
        best = jnp.maximum(best, fastest_of(prims))
        for side, edge in ((0, 0), (1, ny - 1)):
            for f in range(5):
                hy[side, f, pl.ds(x, 1), :] = coarse[f, x, edge : edge + 1, :]
        for side, edge in ((0, 0), (1, nz - 1)):
            for f in range(5):
                column = jnp.broadcast_to(u[f][:, edge : edge + 1], (ny, 128))
                hz[side, f] = jnp.where(lane_tile == x, column, hz[side, f])
        x_inside = jnp.where((x >= SHIFT) & (x < SHIFT + CORE), 1.0, 0.0)
        x_face = jnp.where((x == SHIFT) | (x == SHIFT + CORE), 1.0, 0.0)
        flux, speed = dirflux(u, prims, 0)
        lower = face(
            [coarse[f, before] for f in range(5)], [pflux[f] for f in range(5)], pspeed[...], u, flux, speed
        )
        lower = [jnp.where(x > 0, piece, 0.0) for piece in lower]
        for f in range(5):
            pflux[f] = flux[f]
        pspeed[...] = speed
        keep = 1.0 - x_face * at_x
        lower_l = [piece * keep for piece in lower]
        change = [-piece for piece in lower]
        change_l = [-piece for piece in lower_l]
        for d, axis, size, first, at_lo, at_hi in (
            (1, 0, ny, keep_row, at_y_lo, at_y_hi),
            (2, 1, nz, keep_lane, at_z_lo, at_z_hi),
        ):
            flux, speed = dirflux(u, prims, d)
            ru = [pltpu.roll(piece, 1, axis) for piece in u]
            rf = [ru[1 + d]] + [pltpu.roll(piece, 1, axis) for piece in flux[1:]]
            lo = face(ru, rf, pltpu.roll(speed, 1, axis), u, flux, speed)
            keep_lo = 1.0 - x_inside * at_lo
            keep_hi = 1.0 - x_inside * at_hi
            for f in range(5):
                low = lo[f] * first
                high = pltpu.roll(low, size - 1, axis)
                change[f] = change[f] + (high - low)
                change_l[f] = change_l[f] + (high * keep_hi - low * keep_lo)
        for f in range(5):
            chgf[f, x] = change[f]
            chgl[f, x] = change_l[f]
            chgf[f, before] = chgf[f, before] + lower[f]
            chgl[f, before] = chgl[f, before] + lower_l[f]
        return best

    hz[...] = jnp.zeros_like(hz)
    best = fold(lax.fori_loop(0, nx, plane, jnp.zeros((ny, nz), F32)))

    count = 10 * 32
    for g in range(10):
        src, f = (coarse, g) if g < 5 else (chgf, g - 5)
        outer = (SHIFT - 1, SHIFT + CORE)
        inner = range(SHIFT, SHIFT + CORE)
        on_x = [src[f, x, SHIFT : SHIFT + CORE, :] for x in outer]
        on_y = [src[f, x, y : y + 1, :] for y in outer for x in inner]
        put_split(cxy, g * 32, count, jnp.concatenate(on_x + on_y, axis=0))
        on_z = [src[f, x, SHIFT : SHIFT + CORE, :] for x in inner]
        put_split(cz, g * 64, 640, jnp.concatenate(on_z, axis=0))
    rxy[...] = sum_split(dot_nt(cxy[...], onehot(keys[0:1, :], 512)))
    rz = sum_split(dot_nt(cz[...], onehot(keys[1:2, :], 128)))
    left = lax.broadcasted_iota(jnp.int32, (8, 128), 1) < 64
    left64 = lax.broadcasted_iota(jnp.int32, (64, 128), 1) < 64

    def put(line, tile):
        for part in range(8):
            pay[pl.ds(part * 8 * OUT_ROWS + line, 8, stride=OUT_ROWS), :] = tile[part * 8 : part * 8 + 8]

    for g in range(10):
        pieces = []
        for side in range(2):
            for j in range(CORE):
                lanes = slice(j // 2 * 128, j // 2 * 128 + 128)
                a = rxy[g * 32 + side * 8 : g * 32 + side * 8 + 8, lanes]
                b = rxy[g * 32 + 16 + side * 8 : g * 32 + 24 + side * 8, lanes]
                if j % 2 == 0:
                    pieces.append(jnp.where(left, a, pltpu.roll(b, 64, 1)))
                else:
                    pieces.append(jnp.where(left, pltpu.roll(a, 64, 1), b))
        turned = jnp.concatenate(pieces, axis=0).T
        put(g * 3, turned[:64])
        put(g * 3 + 1, turned[64:])
    for pair in range(5):
        turned = rz[pair * 128 : pair * 128 + 128].T
        a, b = turned[:64], turned[64:]
        put(pair * 6 + 2, jnp.where(left64, a, pltpu.roll(b, 64, 1)))
        put(pair * 6 + 5, jnp.where(left64, pltpu.roll(a, 64, 1), b))
    for line in (30, 31):
        put(line, jnp.zeros((64, 128), F32))

    def fine_plane(p, best):
        at = pl.multiple_of(p * 256, 256)
        u = [fine[:, f, pl.ds(at, 256)] for f in range(5)]
        for f in range(5):
            finet[f, :, pl.ds(at, 256)] = u[f]
        return jnp.maximum(best, fastest_of(speeds(u)))

    fine_best = lax.fori_loop(0, BOX, fine_plane, jnp.zeros((16, 256), F32))
    top[...] = jnp.maximum(best, fold(fine_best))


def plane_peer(s, sign):
    count_x, count_z = lax.axis_size("gx"), lax.axis_size("gz")
    x = lax.rem(lax.axis_index("gx") + sign * (s // count_z) + count_x, count_x)
    z = lax.rem(lax.axis_index("gz") + sign * lax.rem(s, count_z) + count_z, count_z)
    return x, z


def exchange_kernel(halos, *refs):
    if halos:
        (pay, coarse, hy, hz, top, arr, gx, gy, gz, gmax, tops, tops2, mine, send, recv, here, hs, hr, ts, tr, us, ur) = refs
    else:
        pay, arr, send, recv, here = refs
    ix, iy, iz = (lax.axis_index(a) for a in ("gx", "gy", "gz"))
    nx, ny, nz = (lax.axis_size(a) for a in ("gx", "gy", "gz"))
    me = ix * nz + iz
    peers = nx * nz
    barrier = pltpu.get_barrier_semaphore()

    @pl.loop(1, peers)
    def _(s):
        x, z = plane_peer(s, 1)
        pl.semaphore_signal(barrier, inc=1, device_id=(x, iy, z), device_id_type=MESH)

    if halos:

        @pl.loop(1, ny)
        def _(s):
            pl.semaphore_signal(
                barrier, inc=1, device_id=(ix, lax.rem(iy + s, ny), iz), device_id_type=MESH
            )

    pl.semaphore_wait(barrier, peers - 1 + (ny - 1 if halos else 0))

    def remote(src, dst, a, b, device):
        return pltpu.make_async_remote_copy(
            src_ref=src, dst_ref=dst, send_sem=a, recv_sem=b, device_id=device, device_id_type=MESH
        )

    def patch(s):
        x, z = plane_peer(s, 1)
        return remote(pay.at[x * nz + z], arr.at[me], send.at[s], recv.at[s], (x, iy, z))

    if halos:

        def first(s):
            return remote(mine.at[0], tops.at[s], ts.at[s], tr.at[s], (ix, lax.rem(iy + s, ny), iz))

        def second(s):
            x, z = plane_peer(s, 1)
            return remote(mine.at[1], tops2.at[s], us.at[s], ur.at[s], (x, iy, z))

        mine[0] = top[...]

        @pl.loop(1, ny)
        def _(s):
            first(s).start()

        up_x, down_x = lax.rem(ix + 1, nx), lax.rem(ix + nx - 1, nx)
        up_y, down_y = lax.rem(iy + 1, ny), lax.rem(iy + ny - 1, ny)
        up_z, down_z = lax.rem(iz + 1, nz), lax.rem(iz + nz - 1, nz)
        sides = [
            remote(coarse.at[:, coarse.shape[1] - 1], gx.at[0], hs.at[0], hr.at[0], (up_x, iy, iz)),
            remote(coarse.at[:, 0], gx.at[1], hs.at[1], hr.at[1], (down_x, iy, iz)),
            remote(hy.at[1], gy.at[0], hs.at[2], hr.at[2], (ix, up_y, iz)),
            remote(hy.at[0], gy.at[1], hs.at[3], hr.at[3], (ix, down_y, iz)),
            remote(hz.at[1], gz.at[0], hs.at[4], hr.at[4], (ix, iy, up_z)),
            remote(hz.at[0], gz.at[1], hs.at[5], hr.at[5], (ix, iy, down_z)),
        ]
        for side in sides:
            side.start()

    @pl.loop(1, peers)
    def _(s):
        patch(s).start()

    own = pltpu.make_async_copy(pay.at[me], arr.at[me], here.at[0])
    own.start()
    if halos:

        @pl.loop(1, ny)
        def _(s):
            first(s).wait()

        best = mine[0]
        for s in range(1, ny):
            best = jnp.maximum(best, tops[s])
        mine[1] = best

        @pl.loop(1, peers)
        def _(s):
            second(s).start()

        @pl.loop(1, peers)
        def _(s):
            second(s).wait()

        for s in range(1, peers):
            best = jnp.maximum(best, tops2[s])
        gmax[...] = best
        for side in sides:
            side.wait()
    own.wait()

    @pl.loop(1, peers)
    def _(s):
        patch(s).wait()


def fine_tables():
    c = np.arange(128)
    side, high, low = c // 64, c // 8 % 8, c % 8
    q, r = np.arange(256) // 16, np.arange(256) % 16
    half_q, half_r = q // 2, r // 2
    edge_q = np.where(q == 0, 0, np.where(q == 15, 1, -1))
    edge_r = np.where(r == 0, 0, np.where(r == 15, 1, -1))

    def both(*conditions):
        return np.logical_and.reduce(np.broadcast_arrays(*conditions))

    up_x = np.concatenate(
        [
            both(side[:, None] == s, low[:, None] == half_q[None], high[:, None] == half_r[None])
            for s in range(2)
        ],
        axis=1,
    )
    up_y = np.concatenate(
        [
            both(low[:, None] == x, side[:, None] == edge_q[None], high[:, None] == half_r[None])
            for x in range(8)
        ],
        axis=1,
    )
    up_z = np.concatenate(
        [
            both(high[:, None] == x, side[:, None] == edge_r[None], low[:, None] == half_q[None])
            for x in range(8)
        ],
        axis=1,
    )
    pool_a = both(half_q[:, None] == low[None], half_r[:, None] == high[None]) * 0.125
    pool_y = both(edge_q[:, None] == side[None], half_r[:, None] == high[None]) * 0.125
    pool_z = both(edge_r[:, None] == side[None], half_q[:, None] == low[None]) * 0.125
    return [jnp.asarray(t.astype(np.float32), BF16) for t in (up_x, up_y, up_z, pool_a, pool_y, pool_z)]


def fine_kernel(
    box_lane, arr, gmax, finet, ux, uy, uz, pa, py, pz, ret, out,
    fu, g, lhs, gy, gz, rx, ry, rz, big, stage, sems,
):
    copies = [
        pltpu.make_async_copy(finet.at[f], fu.at[f, :, pl.ds(256, 4096)], sems.at[f]) for f in range(5)
    ]
    for copy in copies:
        copy.start()
    courant = COURANT_NUMBER / jnp.max(gmax[...])
    for b in range(16):
        at = pl.multiple_of(box_lane[b] * OUT_ROWS, OUT_ROWS)
        g[pl.ds(b, OUT_ROWS, stride=16), :] = arr[pl.ds(at, OUT_ROWS), :]
    rx[...] = jnp.zeros_like(rx)
    ry[...] = jnp.zeros_like(ry)
    rz[...] = jnp.zeros_like(rz)

    def ghost(part, table):
        for f in range(5):
            old = g[pl.ds((f * 3 + part) * 16, 16), :]
            change = g[pl.ds(((5 + f) * 3 + part) * 16, 16), :]
            put_split(lhs, f * 16, 160, old)
            put_split(lhs, 80 + f * 16, 160, 0.5 * (old + (old - courant * change)))
        return sum_split(dot_nn(lhs[...], table[...]))

    gy[...] = ghost(1, uy)
    gz[...] = ghost(2, uz)
    gx = ghost(0, ux)
    lane = lax.broadcasted_iota(jnp.int32, (8, 256), 1)
    q, r = lane // 16, lane % 16
    for copy in copies:
        copy.wait()
    for sub in range(2):
        for f in range(5):
            fu[f, :, 0:256] = gx[sub * 80 + f * 16 : sub * 80 + f * 16 + 16, :256]
            fu[f, :, 17 * 256 :] = gx[sub * 80 + f * 16 : sub * 80 + f * 16 + 16, 256:]

        @pl.loop(0, 2)
        def _(half):
            rows = pl.ds(pl.multiple_of(half * 8, 8), 8)

            def load(p):
                return [fu[f, rows, pl.ds(pl.multiple_of(p * 256, 256), 256)] for f in range(5)]

            ghost_u = load(0)
            gp = speeds(ghost_u)
            gf, gs = dirflux(ghost_u, gp, 0)
            u0 = load(1)
            p0 = speeds(u0)
            f0, s0 = dirflux(u0, p0, 0)
            start = face(ghost_u, gf, gs, u0, f0, s0)
            for f in range(5):
                rx[f, rows, 0:256] = rx[f, rows, 0:256] + start[f]

            def plane(p, carry):
                u, vel, pressure, sound, lower = carry
                prims = (vel, pressure, sound)
                nxt = load(p + 2)
                nprims = speeds(nxt)
                fx, sx = dirflux(u, prims, 0)
                nf, ns = dirflux(nxt, nprims, 0)
                upper = face(u, fx, sx, nxt, nf, ns)
                change = [a - b for a, b in zip(upper, lower)]
                pair = pl.multiple_of(p // 2 * 256, 256)
                for d, ghosts, regs, coordinate, shift in ((1, gy, ry, q, 16), (2, gz, rz, r, 1)):
                    gu = [
                        ghosts[pl.ds(pl.multiple_of(sub * 80 + f * 16 + half * 8, 8), 8), pl.ds(pair, 256)]
                        for f in range(5)
                    ]
                    fc, sc = dirflux(u, prims, d)
                    first, last = coordinate == 0, coordinate == 15
                    ul = [jnp.where(first, a, pltpu.roll(b, shift, 1)) for a, b in zip(gu, u)]
                    fl, sl = dirflux(ul, speeds(ul), d)
                    lo = face(ul, fl, sl, u, fc, sc)
                    uh = [jnp.where(last, a, b) for a, b in zip(gu, u)]
                    fh, sh = dirflux(uh, speeds(uh), d)
                    top = face(u, fc, sc, uh, fh, sh)
                    for f in range(5):
                        hi = jnp.where(last, top[f], pltpu.roll(lo[f], 256 - shift, 1))
                        change[f] = change[f] + (hi - lo[f])
                        edge = jnp.where(first, lo[f], jnp.where(last, hi, 0.0))
                        regs[f, rows, pl.ds(pair, 256)] = regs[f, rows, pl.ds(pair, 256)] + edge
                for f in range(5):
                    fu[f, rows, pl.ds(pl.multiple_of((p + 1) * 256, 256), 256)] = u[f] - courant * change[f]
                return nxt, nprims[0], nprims[1], nprims[2], upper

            final = lax.fori_loop(0, BOX, plane, (u0, p0[0], p0[1], p0[2], start))
            for f in range(5):
                rx[f, rows, 256:512] = rx[f, rows, 256:512] + final[4][f]

    for f in range(5):
        for p in range(16):
            out[:, f, p * 256 : p * 256 + 256] = fu[f, :, (p + 1) * 256 : (p + 2) * 256]
    ret[...] = jnp.zeros_like(ret)
    tile_lane = lax.broadcasted_iota(jnp.int32, (16, 128), 1)
    left = tile_lane < 64

    def put(line, tile):
        for half in range(2):
            stage[pl.ds(half * 8 * BACK_ROWS + line, 8, stride=BACK_ROWS), :] = tile[half * 8 : half * 8 + 8]

    def pooled(pieces, table):
        count = 16 * len(pieces)
        for i, piece in enumerate(pieces):
            put_split(big, i * 16, count, piece)
        return sum_split(dot_nn(big[pl.ds(0, 3 * count), :], table[...]))

    cells = [
        fu[f, :, (2 * x + 1) * 256 : (2 * x + 2) * 256] + fu[f, :, (2 * x + 2) * 256 : (2 * x + 3) * 256]
        for f in range(5)
        for x in range(8)
    ]
    cells += [rx[f, :, s * 256 : s * 256 + 256] for f in range(5) for s in range(2)]
    done = pooled(cells, pa)
    for f in range(5):
        for i in range(4):
            at = (f * 8 + 2 * i) * 16
            put(f * 7 + i, jnp.where(left, done[at : at + 16], done[at + 16 : at + 32]))
        at = (40 + 2 * f) * 16
        put(f * 7 + 4, jnp.where(left, done[at : at + 16], done[at + 16 : at + 32]))
    for line, regs, table, owner in ((5, ry, py, tile_lane % 8), (6, rz, pz, tile_lane // 8 % 8)):
        done = pooled([regs[f, :, x * 256 : x * 256 + 256] for f in range(5) for x in range(8)], table)
        for f in range(5):
            total = done[f * 128 : f * 128 + 16]
            for x in range(1, 8):
                at = (f * 8 + x) * 16
                total = jnp.where(owner == x, done[at : at + 16], total)
            put(f * 7 + line, total)
    for line in range(35, BACK_ROWS):
        put(line, jnp.zeros((16, 128), F32))
    for b in range(16):
        at = pl.multiple_of(box_lane[b] * BACK_ROWS, BACK_ROWS)
        ret[pl.ds(at, BACK_ROWS), :] = stage[b * BACK_ROWS : (b + 1) * BACK_ROWS, :]


def apply_kernel(coarse, chgl, keys, arr, gmax, gx, gy, gz, hy, hz, out, lxy, lz, dxy, dz):
    nx, ny, nz = coarse.shape[1:]
    courant = COURANT_NUMBER / jnp.max(gmax[...])
    left = lax.broadcasted_iota(jnp.int32, (16, 128), 1) < 64
    left64 = lax.broadcasted_iota(jnp.int32, (64, 128), 1) < 64

    def lanes_of(line):
        return jnp.concatenate(
            [arr[pl.ds(part * 8 * BACK_ROWS + line, 8, stride=BACK_ROWS), :] for part in range(8)], axis=0
        )

    flat = [(f, i) for f in range(5) for i in range(6)]
    for first in range(0, 30, 2):
        pair = flat[first : first + 2]
        turned = jnp.concatenate([lanes_of(f * 7 + i) for f, i in pair], axis=0).T
        for second in range(2):
            pieces = []
            for couple in range(4):
                even = jnp.concatenate(
                    [turned[a * 64 + couple * 16 : a * 64 + couple * 16 + 8] for a in range(2)], axis=0
                )
                odd = jnp.concatenate(
                    [turned[a * 64 + couple * 16 + 8 : a * 64 + couple * 16 + 16] for a in range(2)], axis=0
                )
                if second == 0:
                    pieces.append(jnp.where(left, even, pltpu.roll(odd, 64, 1)))
                else:
                    pieces.append(jnp.where(left, pltpu.roll(even, 64, 1), odd))
            put_split(lxy, (first + second) * 16, 480, jnp.concatenate(pieces, axis=1))
    for f in range(5):
        both = jnp.concatenate([lanes_of(f * 7 + 6), lanes_of(f * 7 + 6)], axis=0).T
        put_split(lz, f * 64, 320, jnp.where(left64, both[:64], both[64:]))
    dxy[...] = sum_split(dot_nn(lxy[...], onehot(keys[0:1, :], 512)))
    dz[...] = sum_split(dot_nn(lz[...], onehot(keys[1:2, :], 128)))

    def edge(lower, upper, d):
        fl, sl = dirflux(lower, speeds(lower), d)
        fu, su = dirflux(upper, speeds(upper), d)
        return face(lower, fl, sl, upper, fu, su)

    def take(ref, *index):
        return [ref[index[:1] + (f,) + index[1:]] for f in range(5)]

    spot = lax.broadcasted_iota(jnp.int32, (CORE, nz), 1) % BOX
    refined = jnp.broadcast_to(keys[2:3, :], (CORE, nz)) >= 0
    inside = refined & (spot >= SHIFT) & (spot < SHIFT + CORE)
    z_sign = courant * jnp.where(spot == SHIFT - 1, -1.0, jnp.where(spot == SHIFT + CORE, 1.0, 0.0))
    mid = slice(SHIFT, SHIFT + CORE)
    for f in range(5):
        for x in range(nx):
            out[f, x] = coarse[f, x] - courant * chgl[f, x]
        for side, x, sign in ((0, SHIFT - 1, -1.0), (1, SHIFT + CORE, 1.0)):
            at = (f * 6 + 4) * 16 + side * 8
            out[f, x, mid, :] = out[f, x, mid, :] + (sign * courant) * dxy[at : at + 8, :]
            at = (f * 6 + 5) * 16 + side * 8
            for i in range(CORE):
                y = x
                out[f, SHIFT + i, y : y + 1, :] = (
                    out[f, SHIFT + i, y : y + 1, :] + (sign * courant) * dxy[at + i : at + i + 1, :]
                )
        for i in range(CORE):
            fixed = out[f, SHIFT + i, mid, :] + z_sign * dz[f * 64 + i * 8 : f * 64 + i * 8 + 8, :]
            average = dxy[f * 96 + i * 8 : f * 96 + i * 8 + 8, :]
            out[f, SHIFT + i, mid, :] = jnp.where(inside, average, fixed)

    low = edge([gx[0, f] for f in range(5)], [coarse[f, 0] for f in range(5)], 0)
    high = edge([coarse[f, nx - 1] for f in range(5)], [gx[1, f] for f in range(5)], 0)
    for f in range(5):
        out[f, 0] = out[f, 0] + courant * low[f]
        out[f, nx - 1] = out[f, nx - 1] - courant * high[f]
    low = edge(take(gy, 0), take(hy, 0), 1)
    high = edge(take(hy, 1), take(gy, 1), 1)
    for f in range(5):
        for x in range(nx):
            out[f, x, 0:1, :] = out[f, x, 0:1, :] + courant * low[f][x : x + 1]
            out[f, x, ny - 1 : ny, :] = out[f, x, ny - 1 : ny, :] - courant * high[f][x : x + 1]
    tile = lax.broadcasted_iota(jnp.int32, (ny, 128), 1)
    real = tile < nx

    def cells(ref, side):
        return [jnp.where(real, ref[side, f], 1.0) for f in range(5)]

    low = edge(cells(gz, 0), cells(hz, 0), 2)
    high = edge(cells(hz, 1), cells(gz, 1), 2)
    for f in range(5):
        for x in range(nx):
            add = jnp.broadcast_to(courant * low[f][:, x : x + 1], (ny, 128))
            out[f, x, :, 0:128] = out[f, x, :, 0:128] + jnp.where(tile == 0, add, 0.0)
            add = jnp.broadcast_to(courant * high[f][:, x : x + 1], (ny, 128))
            out[f, x, :, nz - 128 :] = out[f, x, :, nz - 128 :] - jnp.where(tile == 127, add, 0.0)


VMEM = pl.BlockSpec(memory_space=pltpu.VMEM)
SMEM = pl.BlockSpec(memory_space=pltpu.SMEM)
ANY = pl.BlockSpec(memory_space=pl.ANY)


def shape(*dims):
    return jax.ShapeDtypeStruct(dims, F32)


def coarse_call(coarse, keys, fine):
    _, nx, ny, nz = coarse.shape
    return pl.pallas_call(
        coarse_kernel,
        out_shape=[
            shape(64 * OUT_ROWS, 128),
            shape(5, nx, ny, nz),
            shape(2, 5, nx, nz),
            shape(2, 5, ny, 128),
            shape(5, 16, 4096),
            shape(8, 128),
        ],
        in_specs=[VMEM, VMEM, VMEM],
        out_specs=[VMEM] * 6,
        scratch_shapes=[
            pltpu.VMEM((5, nx, ny, nz), F32),
            pltpu.VMEM((5, ny, nz), F32),
            pltpu.VMEM((ny, nz), F32),
            pltpu.VMEM((960, nz), BF16),
            pltpu.VMEM((1920, nz), BF16),
            pltpu.VMEM((320, 512), F32),
        ],
        compiler_params=pltpu.CompilerParams(vmem_limit_bytes=VMEM_LIMIT),
        name="coarse_flux_pack",
    )(coarse, keys, fine)


def exchange_call(pay, halos):
    peers = lax.axis_size("gx") * lax.axis_size("gz")
    count_y = lax.axis_size("gy")
    dma = pltpu.SemaphoreType.DMA
    own = [dma((peers,)), dma((peers,)), dma((1,))]
    if halos is None:
        return pl.pallas_call(
            functools.partial(exchange_kernel, False),
            out_shape=shape(*pay.shape),
            in_specs=[ANY],
            out_specs=ANY,
            scratch_shapes=own,
            compiler_params=pltpu.CompilerParams(
                collective_id=1, has_side_effects=True, vmem_limit_bytes=VMEM_LIMIT
            ),
            name="return_exchange",
        )(pay)
    coarse, hy, hz, top = halos
    return pl.pallas_call(
        functools.partial(exchange_kernel, True),
        out_shape=[
            shape(*pay.shape),
            shape(2, 5, coarse.shape[2], coarse.shape[3]),
            shape(*hy.shape),
            shape(*hz.shape),
            shape(8, 128),
        ],
        in_specs=[ANY, ANY, ANY, ANY, VMEM],
        out_specs=[ANY, ANY, ANY, ANY, VMEM],
        scratch_shapes=[
            pltpu.VMEM((count_y, 8, 128), F32),
            pltpu.VMEM((peers, 8, 128), F32),
            pltpu.VMEM((2, 8, 128), F32),
            *own,
            dma((6,)),
            dma((6,)),
            dma((count_y,)),
            dma((count_y,)),
            dma((peers,)),
            dma((peers,)),
        ],
        compiler_params=pltpu.CompilerParams(
            collective_id=0, has_side_effects=True, vmem_limit_bytes=VMEM_LIMIT
        ),
        name="patch_exchange",
    )(pay, coarse, hy, hz, top)


def fine_call(box_lane, arr, gmax, finet):
    tables = fine_tables()
    return pl.pallas_call(
        fine_kernel,
        out_shape=[shape(64 * BACK_ROWS, 128), shape(16, 5, 4096)],
        in_specs=[SMEM, VMEM, VMEM, ANY] + [VMEM] * 6,
        out_specs=[VMEM, VMEM],
        scratch_shapes=[
            pltpu.VMEM((5, 16, 18 * 256), F32),
            pltpu.VMEM((16 * OUT_ROWS, 128), F32),
            pltpu.VMEM((480, 128), BF16),
            pltpu.VMEM((160, 2048), F32),
            pltpu.VMEM((160, 2048), F32),
            pltpu.VMEM((5, 16, 512), F32),
            pltpu.VMEM((5, 16, 2048), F32),
            pltpu.VMEM((5, 16, 2048), F32),
            pltpu.VMEM((2400, 256), BF16),
            pltpu.VMEM((16 * BACK_ROWS, 128), F32),
            pltpu.SemaphoreType.DMA((5,)),
        ],
        compiler_params=pltpu.CompilerParams(vmem_limit_bytes=VMEM_LIMIT),
        name="fine_boxes",
    )(box_lane, arr, gmax, finet, *tables)


def apply_call(coarse, chgl, keys, arr, gmax, gx, gy, gz, hy, hz):
    nz = coarse.shape[3]
    return pl.pallas_call(
        apply_kernel,
        out_shape=shape(*coarse.shape),
        in_specs=[VMEM] * 10,
        out_specs=VMEM,
        scratch_shapes=[
            pltpu.VMEM((1440, 512), BF16),
            pltpu.VMEM((960, 128), BF16),
            pltpu.VMEM((480, nz), F32),
            pltpu.VMEM((320, nz), F32),
        ],
        compiler_params=pltpu.CompilerParams(vmem_limit_bytes=VMEM_LIMIT),
        name="reflux_apply",
    )(coarse, chgl, keys, arr, gmax, gx, gy, gz, hy, hz)


def tables_of(slot_owner, box_corner, count_gz):
    owners = slot_owner.reshape(-1)
    slots = owners.shape[0]
    index = jnp.arange(slots, dtype=jnp.int32)
    rank = jnp.sum(
        (owners[:, None] == owners[None, :]) & (index[None, :] < index[:, None]), axis=1, dtype=jnp.int32
    )
    slot_lane = jnp.where(owners >= 0, owners * 2 + rank, -1)
    lane_z = jnp.repeat(slot_lane, BOX)
    spot = jnp.arange(slots * BOX, dtype=jnp.int32) % BOX
    on = lane_z >= 0
    inner = on & (spot >= SHIFT) & (spot < SHIFT + CORE)
    outer = on & ((spot == SHIFT - 1) | (spot == SHIFT + CORE))
    key_xy = jnp.where(inner, (spot - SHIFT) * 64 + lane_z, -1)
    key_z = jnp.where(outer, jnp.where(spot < SHIFT, 0, 64) + lane_z, -1)
    keys = jnp.stack([key_xy, key_z, lane_z] + [lane_z] * 5)
    source = box_corner[:, 0] * count_gz + box_corner[:, 2] // slots
    number = jnp.arange(source.shape[0], dtype=jnp.int32)
    place = jnp.sum(
        (source[:, None] == source[None, :]) & (number[None, :] < number[:, None]), axis=1, dtype=jnp.int32
    )
    return keys, source * 2 + place


def local(coarse_old, fine_old, slot_owner, box_corner):
    peers = lax.axis_size("gx") * lax.axis_size("gz")
    keys, box_lane = tables_of(slot_owner, box_corner, lax.axis_size("gz"))
    pay, chgl, hy, hz, finet, top = coarse_call(coarse_old, keys, fine_old)
    arr, gx, gy, gz, gmax = exchange_call(pay.reshape(peers, -1, 128), (coarse_old, hy, hz, top))
    ret, fine_new = fine_call(box_lane, arr.reshape(-1, 128), gmax, finet)
    back = exchange_call(ret.reshape(peers, -1, 128), None)
    coarse_new = apply_call(
        coarse_old, chgl, keys, back.reshape(-1, 128), gmax, gx, gy, gz, hy, hz
    )
    return (coarse_new, fine_new)


def solution(mesh):
    in_specs = (
        P(None, "gx", "gy", "gz"),
        P(("gx", "gy", "gz"), None, None),
        P("gx", "gy", "gz"),
        P(("gx", "gy", "gz"), None),
    )
    out_specs = (P(None, "gx", "gy", "gz"), P(("gx", "gy", "gz"), None, None))
    return jax.shard_map(local, mesh=mesh, in_specs=in_specs, out_specs=out_specs, check_vma=False)
```

time: 860 us -> 131 us (0.15)
  local copies, waits for them, and re-layouts: 490 us -> 6.05 us
  other arithmetic: 175 us -> 4.6 us
  Pallas kernels: 0 us -> 119 us
  waiting for transfers between devices: 79.5 us -> 0 us
  blocking collectives: 78.4 us -> 0 us
  starting transfers between devices: 21.7 us -> 0 us
    gather x41 -> x0, local copies, waits for them, and re-layouts: 197 us -> none  [the longest x4 55.3 us: fine_step(): jnp.take(jnp.take(coarse_now, jnp.asarray(ghost_x), axis=2), jnp.asarray(...]
    pallas_call x0 -> x5, Pallas kernels: none -> 119 us  [the longest x1 40.9 us: exchange_call(): pl.pallas_call(functools.partial(exchange_kernel, True), out_shape=[shape...]
    all_to_all x2 -> x0, waiting for transfers between devices: 79.2 us -> none  [across(): lax.all_to_all(buffer, ('gx', 'gz'), split_axis=0, concat_axis=0, tiled=T...]
    pmax x1 -> x0, blocking collectives: 78.4 us -> none  [local(): fastest = lax.pmax(local_top, ('gx', 'gy', 'gz'))]
    slice x36 -> x0, local copies, waits for them, and re-layouts: 71 us -> none  [the longest x4 22.8 us: fine_step(): flux_z[:, :, 1:BOX + 1]]
    unnamed x508 -> x4, local copies, waits for them, and re-layouts: 72.6 us -> 5.27 us
    reshape x14 -> x1, local copies, waits for them, and re-layouts: 50.4 us -> 0.08 us  [tables_of(): lane_z = jnp.repeat(slot_lane, BOX)]
    unnamed x84 -> x0, other arithmetic: 43.3 us -> none
  transfers between devices with their start and end apart: 8 -> 0, of which waited for: 3 -> 0; matrix products, arithmetic and copies ran while one was open for 26% -> 0% of each run, Pallas kernels for 0% -> 0%
where the time goes in v1:
time: 131 us; the launch traced here: 130 us
  Pallas kernels  119 us (91%)
  local copies, waits for them, and re-layouts  6.05 us (5%)
  other arithmetic  4.6 us (4%)
    pallas_call x1, Pallas kernels, exchange_call(): pl.pallas_call(functools.partial(exchange_kernel, True), out_shape=[shape...  40.9 us
    pallas_call x1, Pallas kernels, exchange_call(): pl.pallas_call(functools.partial(exchange_kernel, False), out_shape=shape...  36.5 us
    pallas_call x1, Pallas kernels, fine_call(): pl.pallas_call(fine_kernel, out_shape=[shape(64 * BACK_ROWS, 128), shape(...  19.2 us
    pallas_call x1, Pallas kernels, coarse_call(): pl.pallas_call(coarse_kernel, out_shape=[shape(64 * OUT_ROWS, 128), shape...  15.2 us
    pallas_call x1, Pallas kernels, apply_call(): pl.pallas_call(apply_kernel, out_shape=shape(*coarse.shape), in_specs=[VM...  7.21 us
    unnamed x4, local copies, waits for them, and re-layouts  5.27 us

profile of v1, /device:TPU:4, one launch (start us, length us, event | category | flops | bytes accessed | tf_op | source)
XLA Modules:
  0.0 130.3 jit_solution(15221046101387537325)
XLA Ops:
  0.6 0.9 convert_reduce_fusion
  1.5 0.7 compare_select_fusion.1
  2.2 0.8 bitcast_add_fusion
  3.0 0.8 add_bitcast_fusion
  3.7 0.2 convert_reduce_fusion.1
  3.9 1.3 multiply_add_fusion.box_lane
  5.2 0.1 broadcast_in_dim.23
  5.3 0.1 reshape.158
  5.4 0.6 stack.2.keys
  6.0 3.4 %copy.16.fine = f32[16,5,4096]{2,1,0:T(8,128)} copy(f32[16,5,4096]{2,0,1:T(8,128)} %param.11) | data formatting | bytes 2621440 | tf_op args[1]
  9.5 15.2 %coarse_flux_pack.1 = (f32[2048,128]{1,0:T(8,128)}, f32[5,16,16,512]{3,2,1,0:T(8,128)}, f32[2,5,16,512]{3,2,1,0:T(8,128)}, f32[2,5,16,128]{3,2,1,0:T(8,128)}, f32[5,16,4096]{2,1,0:T(8,128)}, /*index=5*/f32[8,128]{1,0:T(8,128)}) custom-call(f32[5,16,16,512]{3,2,1,0:T(8,128)} %coarse.3, s32[8,512]{1,0:T(8,128)} %stack.2.keys, f32[16,5,4096]{2,1,0:T(8,128)} %copy.16.fine), custom_call_target="tpu_custom_call" | custom-call | tf_op jit(solution)/shard_map/coarse_flux_pack/pallas_call | solution.py:603
  24.7 40.9 %patch_exchange.1 = (f32[32,64,128]{2,1,0:T(8,128)}, f32[2,5,16,512]{3,2,1,0:T(8,128)}, f32[2,5,16,512]{3,2,1,0:T(8,128)}, f32[2,5,16,128]{3,2,1,0:T(8,128)}, f32[8,128]{1,0:T(8,128)}) custom-call(f32[32,64,128]{2,1,0:T(8,128)} %bitcast.27, f32[5,16,16,512]{3,2,1,0:T(8,128)} %coarse.3, f32[2,5,16,512]{3,2,1,0:T(8,128)} %get-tuple-element.17.refs_2_.hy, ...), custom_call_target="tpu_custom_call" | custom-call | tf_op jit(solution)/shard_map/patch_exchange/pallas_call | solution.py:646
  65.6 19.2 %fine_boxes.1 = (f32[2560,128]{1,0:T(8,128)}, f32[16,5,4096]{2,1,0:T(8,128)}) custom-call(s32[16]{0:T(128)} %multiply_add_fusion.box_lane, f32[2048,128]{1,0:T(8,128)} %bitcast.26, f32[8,128]{1,0:T(8,128)} %get-tuple-element.21.gmax, f32[5,16,4096]{2,1,0:T(8,128)} %get-tuple-element.22.finet, bf16[128,512]{1,0:T(8,128)(2,1)} %constant.63.clone.ux, ...), custom_call_target="tpu_custom_call" | custom-call | tf_op jit(solution)/shard_map/fine_boxes/pallas_call | solution.py:678
  84.8 36.5 %return_exchange.1 = f32[32,80,128]{2,1,0:T(8,128)} custom-call(f32[32,80,128]{2,1,0:T(8,128)} %bitcast.25), custom_call_target="tpu_custom_call" | custom-call | tf_op jit(solution)/shard_map/return_exchange/pallas_call | solution.py:634
  121.3 0.0 copy-start
  121.3 7.2 %reflux_apply.1 = f32[5,16,16,512]{3,2,1,0:T(8,128)} custom-call(f32[5,16,16,512]{3,2,1,0:T(8,128)} %coarse.3, f32[5,16,16,512]{3,2,1,0:T(8,128)} %get-tuple-element.15.chgl, s32[8,512]{1,0:T(8,128)} %stack.2.keys, f32[2560,128]{1,0:T(8,128)} %bitcast.24, f32[8,128]{1,0:T(8,128)} %get-tuple-element.21.gmax, f32[2,5,16,512]{3,2,1,0:T(8,128)} %get-tuple-element.24.gx, ...), custom_call_target="tpu_custom_call" | custom-call | tf_op jit(solution)/shard_map/reflux_apply/pallas_call | solution.py:703
  128.5 0.0 copy-done
  128.5 1.8 %copy.17 = f32[16,5,4096]{2,0,1:T(8,128)} copy(f32[16,5,4096]{2,1,0:T(8,128)S(1)} %copy-done) | data formatting | bytes 2621440
  (1 shorter events, 0.0 us)
Async XLA Ops:
  121.3 7.2 %copy-start = (f32[16,5,4096]{2,1,0:T(8,128)S(1)}, f32[16,5,4096]{2,1,0:T(8,128)}, u32[]{:S(2)}) copy-start(f32[16,5,4096]{2,1,0:T(8,128)} %get-tuple-element.33) | copy-start | bytes 3932164

commit v2 on v1

v2 whole, which is shorter than its diff:
```python
import functools

import jax
import jax.numpy as jnp
import numpy as np
from jax import lax
from jax.experimental import pallas as pl
from jax.experimental.pallas import tpu as pltpu
from jax.sharding import PartitionSpec as P

BOX = 16
CORE = 8
SHIFT = 4
HEAT_RATIO = 1.4
COURANT_NUMBER = 0.15
OUT_ROWS = 16
BACK_ROWS = 36
STAGE_ROWS = 40
MESH = pl.DeviceIdType.MESH
F32 = jnp.float32
BF16 = jnp.bfloat16
VMEM_LIMIT = 56 * 1024 * 1024


def speeds(u):
    inverse = 1.0 / u[0]
    velocity = [u[1] * inverse, u[2] * inverse, u[3] * inverse]
    kinetic = 0.5 * (u[1] * velocity[0] + u[2] * velocity[1] + u[3] * velocity[2])
    pressure = (HEAT_RATIO - 1.0) * (u[4] - kinetic)
    sound = jnp.sqrt(HEAT_RATIO * pressure * inverse)
    return velocity, pressure, sound


def dirflux(u, prims, d):
    velocity, pressure, sound = prims
    normal = velocity[d]
    flux = [u[1 + d]]
    for m in range(3):
        piece = u[1 + m] * normal
        flux.append(piece + pressure if m == d else piece)
    flux.append((u[4] + pressure) * normal)
    return flux, jnp.abs(normal) + sound


def face(ul, fl, sl, ur, fr, sr):
    half = 0.5 * jnp.maximum(sl, sr)
    return [0.5 * (a + b) - half * (d - c) for a, b, c, d in zip(fl, fr, ul, ur)]


def fastest_of(prims):
    velocity, _, sound = prims
    top = jnp.maximum(jnp.abs(velocity[0]), jnp.abs(velocity[1]))
    return jnp.maximum(top, jnp.abs(velocity[2])) + sound


def fold(top):
    best = None
    for row in range(0, top.shape[0], 8):
        for lane in range(0, top.shape[1], 128):
            tile = top[row : row + 8, lane : lane + 128]
            best = tile if best is None else jnp.maximum(best, tile)
    return best


def split3(x):
    high = x.astype(BF16)
    rest = x - high.astype(F32)
    middle = rest.astype(BF16)
    low = (rest - middle.astype(F32)).astype(BF16)
    return high, middle, low


def put_split(ref, row, count, x):
    for part, piece in enumerate(split3(x)):
        ref[pl.ds(part * count + row, x.shape[0]), :] = piece


def sum_split(product):
    count = product.shape[0] // 3
    return product[:count] + product[count : 2 * count] + product[2 * count :]


def dot_nt(a, b):
    return lax.dot_general(a, b, (((1,), (1,)), ((), ())), preferred_element_type=F32)


def dot_nn(a, b):
    return lax.dot_general(a, b, (((1,), (0,)), ((), ())), preferred_element_type=F32)


def onehot(key_row, rows):
    index = lax.broadcasted_iota(jnp.int32, (rows, key_row.shape[1]), 0)
    return jnp.where(index == key_row, 1.0, 0.0).astype(BF16)


def fine_tables():
    c = np.arange(128)
    side, high, low = c // 64, c // 8 % 8, c % 8
    q, r = np.arange(256) // 16, np.arange(256) % 16
    half_q, half_r = q // 2, r // 2
    edge_q = np.where(q == 0, 0, np.where(q == 15, 1, -1))
    edge_r = np.where(r == 0, 0, np.where(r == 15, 1, -1))

    def both(*conditions):
        return np.logical_and.reduce(np.broadcast_arrays(*conditions))

    up_x = np.concatenate(
        [
            both(side[:, None] == s, low[:, None] == half_q[None], high[:, None] == half_r[None])
            for s in range(2)
        ],
        axis=1,
    )
    up_y = np.concatenate(
        [
            both(low[:, None] == x, side[:, None] == edge_q[None], high[:, None] == half_r[None])
            for x in range(8)
        ],
        axis=1,
    )
    up_z = np.concatenate(
        [
            both(high[:, None] == x, side[:, None] == edge_r[None], low[:, None] == half_q[None])
            for x in range(8)
        ],
        axis=1,
    )
    pool_a = both(half_q[:, None] == low[None], half_r[:, None] == high[None]) * 0.125
    pool_y = both(edge_q[:, None] == side[None], half_r[:, None] == high[None]) * 0.125
    pool_z = both(edge_r[:, None] == side[None], half_q[:, None] == low[None]) * 0.125
    return [jnp.asarray(t.astype(np.float32), BF16) for t in (up_x, up_y, up_z, pool_a, pool_y, pool_z)]


def plane_peer(s, sign):
    count_x, count_z = lax.axis_size("gx"), lax.axis_size("gz")
    x = lax.rem(lax.axis_index("gx") + sign * (s // count_z) + count_x, count_x)
    z = lax.rem(lax.axis_index("gz") + sign * lax.rem(s, count_z) + count_z, count_z)
    return x, z


def remote(src, dst, send, recv, device):
    return pltpu.make_async_remote_copy(
        src_ref=src, dst_ref=dst, send_sem=send, recv_sem=recv, device_id=device, device_id_type=MESH
    )


def lanes_of_peer(peer, rows):
    return pl.ds(pl.multiple_of(peer * 2 * rows, 8), 2 * rows)


def start_patches(pay, arr, rows, send, recv):
    iy = lax.axis_index("gy")
    me = lax.axis_index("gx") * lax.axis_size("gz") + lax.axis_index("gz")

    def patch(s):
        x, z = plane_peer(s, 1)
        peer = x * lax.axis_size("gz") + z
        return remote(
            pay.at[lanes_of_peer(peer, rows), :], arr.at[lanes_of_peer(me, rows), :], send.at[s], recv.at[s], (x, iy, z)
        )

    @pl.loop(1, lax.axis_size("gx") * lax.axis_size("gz"))
    def _(s):
        patch(s).start()

    return patch


def pack(fields, keys_z, exy, pay, cxy, cz, rxy):
    outer = (SHIFT - 1, SHIFT + CORE)
    inner = range(SHIFT, SHIFT + CORE)
    for f in range(5):
        on_x = [fields[f, x, SHIFT : SHIFT + CORE, :] for x in outer]
        on_y = [fields[f, x, y : y + 1, :] for y in outer for x in inner]
        put_split(cxy, f * 32, 160, jnp.concatenate(on_x + on_y, axis=0))
        on_z = [fields[f, x, SHIFT : SHIFT + CORE, :] for x in inner]
        put_split(cz, f * 64, 320, jnp.concatenate(on_z, axis=0))
    rxy[...] = sum_split(dot_nt(cxy[...], exy[...]))
    rz = sum_split(dot_nt(cz[...], onehot(keys_z, 128)))
    left = lax.broadcasted_iota(jnp.int32, (8, 128), 1) < 64
    left64 = lax.broadcasted_iota(jnp.int32, (64, 128), 1) < 64

    def put(line, tile):
        for part in range(8):
            pay[pl.ds(part * 8 * OUT_ROWS + line, 8, stride=OUT_ROWS), :] = tile[part * 8 : part * 8 + 8]

    for f in range(5):
        pieces = []
        for side in range(2):
            for j in range(CORE):
                lanes = slice(j // 2 * 128, j // 2 * 128 + 128)
                a = rxy[f * 32 + side * 8 : f * 32 + side * 8 + 8, lanes]
                b = rxy[f * 32 + 16 + side * 8 : f * 32 + 24 + side * 8, lanes]
                if j % 2 == 0:
                    pieces.append(jnp.where(left, a, pltpu.roll(b, 64, 1)))
                else:
                    pieces.append(jnp.where(left, pltpu.roll(a, 64, 1), b))
        turned = jnp.concatenate(pieces, axis=0).T
        put(f * 3, turned[:64])
        put(f * 3 + 1, turned[64:])
        turned = rz[f * 64 : f * 64 + 64]
        turned = jnp.concatenate([turned, turned], axis=0).T
        put(f * 3 + 2, jnp.where(left64, turned[:64], turned[64:]))


def coarse_changes(coarse, refined_row, chgf, chgl, pflux, pspeed, hy, hz):
    nx, ny, nz = coarse.shape[1:]
    row = lax.broadcasted_iota(jnp.int32, (ny, nz), 0)
    lane = lax.broadcasted_iota(jnp.int32, (ny, nz), 1)
    spot = lane % BOX
    refined = jnp.broadcast_to(refined_row, (ny, nz)) >= 0
    row_in = (row >= SHIFT) & (row < SHIFT + CORE)
    lane_in = refined & (spot >= SHIFT) & (spot < SHIFT + CORE)

    def mark(mask):
        return jnp.where(mask, 1.0, 0.0)

    at_x = mark(row_in & lane_in)
    at_y_lo = mark(lane_in & ((row == SHIFT) | (row == SHIFT + CORE)))
    at_y_hi = mark(lane_in & ((row == SHIFT - 1) | (row == SHIFT + CORE - 1)))
    at_z_lo = mark(refined & row_in & ((spot == SHIFT) | (spot == SHIFT + CORE)))
    at_z_hi = mark(refined & row_in & ((spot == SHIFT - 1) | (spot == SHIFT + CORE - 1)))
    keep_row = mark(row > 0)
    keep_lane = mark(lane > 0)
    lane_tile = lax.broadcasted_iota(jnp.int32, (ny, 128), 1)

    def plane(x, best):
        before = jnp.maximum(x - 1, 0)
        u = [coarse[f, x] for f in range(5)]
        prims = speeds(u)
        best = jnp.maximum(best, fastest_of(prims))
        for side, edge in ((0, 0), (1, ny - 1)):
            for f in range(5):
                hy[side, f, pl.ds(x, 1), :] = coarse[f, x, edge : edge + 1, :]
        for side, edge in ((0, 0), (1, nz - 1)):
            for f in range(5):
                column = jnp.broadcast_to(u[f][:, edge : edge + 1], (ny, 128))
                hz[side, f] = jnp.where(lane_tile == x, column, hz[side, f])
        x_inside = jnp.where((x >= SHIFT) & (x < SHIFT + CORE), 1.0, 0.0)
        x_face = jnp.where((x == SHIFT) | (x == SHIFT + CORE), 1.0, 0.0)
        flux, speed = dirflux(u, prims, 0)
        lower = face(
            [coarse[f, before] for f in range(5)], [pflux[f] for f in range(5)], pspeed[...], u, flux, speed
        )
        lower = [jnp.where(x > 0, piece, 0.0) for piece in lower]
        for f in range(5):
            pflux[f] = flux[f]
        pspeed[...] = speed
        keep = 1.0 - x_face * at_x
        lower_l = [piece * keep for piece in lower]
        change = [-piece for piece in lower]
        change_l = [-piece for piece in lower_l]
        for d, axis, size, first, at_lo, at_hi in (
            (1, 0, ny, keep_row, at_y_lo, at_y_hi),
            (2, 1, nz, keep_lane, at_z_lo, at_z_hi),
        ):
            flux, speed = dirflux(u, prims, d)
            ru = [pltpu.roll(piece, 1, axis) for piece in u]
            rf = [ru[1 + d]] + [pltpu.roll(piece, 1, axis) for piece in flux[1:]]
            lo = face(ru, rf, pltpu.roll(speed, 1, axis), u, flux, speed)
            keep_lo = 1.0 - x_inside * at_lo
            keep_hi = 1.0 - x_inside * at_hi
            for f in range(5):
                low = lo[f] * first
                high = pltpu.roll(low, size - 1, axis)
                change[f] = change[f] + (high - low)
                change_l[f] = change_l[f] + (high * keep_hi - low * keep_lo)
        for f in range(5):
            chgf[f, x] = change[f]
            chgl[f, x] = change_l[f]
            chgf[f, before] = chgf[f, before] + lower[f]
            chgl[f, before] = chgl[f, before] + lower_l[f]
        return best

    hz[...] = jnp.zeros_like(hz)
    pflux[...] = jnp.zeros_like(pflux)
    pspeed[...] = jnp.zeros_like(pspeed)
    return fold(lax.fori_loop(0, nx, plane, jnp.zeros((ny, nz), F32)))


def coarse_base(coarse, chgl, courant, gx, gy, gz, hy, hz):
    nx, ny, nz = coarse.shape[1:]

    @pl.loop(0, nx)
    def _(x):
        for f in range(5):
            chgl[f, x] = coarse[f, x] - courant * chgl[f, x]

    def edge(lower, upper, d):
        fl, sl = dirflux(lower, speeds(lower), d)
        fu, su = dirflux(upper, speeds(upper), d)
        return face(lower, fl, sl, upper, fu, su)

    def take(ref, side):
        return [ref[side, f] for f in range(5)]

    low = edge(take(gx, 0), [coarse[f, 0] for f in range(5)], 0)
    high = edge([coarse[f, nx - 1] for f in range(5)], take(gx, 1), 0)
    for f in range(5):
        chgl[f, 0] = chgl[f, 0] + courant * low[f]
        chgl[f, nx - 1] = chgl[f, nx - 1] - courant * high[f]
    low = edge(take(gy, 0), take(hy, 0), 1)
    high = edge(take(hy, 1), take(gy, 1), 1)
    for f in range(5):
        for x in range(nx):
            chgl[f, x, 0:1, :] = chgl[f, x, 0:1, :] + courant * low[f][x : x + 1]
            chgl[f, x, ny - 1 : ny, :] = chgl[f, x, ny - 1 : ny, :] - courant * high[f][x : x + 1]
    tile = lax.broadcasted_iota(jnp.int32, (ny, 128), 1)

    def cells(ref, side):
        return [jnp.where(tile < nx, ref[side, f], 1.0) for f in range(5)]

    low = edge(cells(gz, 0), cells(hz, 0), 2)
    high = edge(cells(hz, 1), cells(gz, 1), 2)
    for f in range(5):
        for x in range(nx):
            add = jnp.broadcast_to(courant * low[f][:, x : x + 1], (ny, 128))
            chgl[f, x, :, 0:128] = chgl[f, x, :, 0:128] + jnp.where(tile == 0, add, 0.0)
            add = jnp.broadcast_to(courant * high[f][:, x : x + 1], (ny, 128))
            chgl[f, x, :, nz - 128 :] = chgl[f, x, :, nz - 128 :] - jnp.where(tile == 127, add, 0.0)


def fine_steps(courant, g_o, g_c, ux, uy, uz, fu, lhs, ghost_y, ghost_z, rx, ry, rz):
    rx[...] = jnp.zeros_like(rx)
    ry[...] = jnp.zeros_like(ry)
    rz[...] = jnp.zeros_like(rz)

    def ghost(part, table):
        for f in range(5):
            old = g_o[pl.ds((f * 3 + part) * 16, 16), :]
            change = g_c[pl.ds((f * 3 + part) * 16, 16), :]
            put_split(lhs, f * 16, 160, old)
            put_split(lhs, 80 + f * 16, 160, 0.5 * (old + (old - courant * change)))
        return sum_split(dot_nn(lhs[...], table[...]))

    ghost_y[...] = ghost(1, uy)
    ghost_z[...] = ghost(2, uz)
    ghost_x = ghost(0, ux)
    lane = lax.broadcasted_iota(jnp.int32, (8, 256), 1)
    q, r = lane // 16, lane % 16
    for sub in range(2):
        for f in range(5):
            fu[f, :, 0:256] = ghost_x[sub * 80 + f * 16 : sub * 80 + f * 16 + 16, :256]
            fu[f, :, 17 * 256 :] = ghost_x[sub * 80 + f * 16 : sub * 80 + f * 16 + 16, 256:]

        @pl.loop(0, 2)
        def _(half):
            rows = pl.ds(pl.multiple_of(half * 8, 8), 8)

            def load(p):
                return [fu[f, rows, pl.ds(pl.multiple_of(p * 256, 256), 256)] for f in range(5)]

            ghost_u = load(0)
            gp = speeds(ghost_u)
            gf, gs = dirflux(ghost_u, gp, 0)
            u0 = load(1)
            p0 = speeds(u0)
            f0, s0 = dirflux(u0, p0, 0)
            start = face(ghost_u, gf, gs, u0, f0, s0)
            for f in range(5):
                rx[f, rows, 0:256] = rx[f, rows, 0:256] + start[f]

            def plane(p, carry):
                u, vel, pressure, sound, lower = carry
                prims = (vel, pressure, sound)
                nxt = load(p + 2)
                nprims = speeds(nxt)
                fx, sx = dirflux(u, prims, 0)
                nf, ns = dirflux(nxt, nprims, 0)
                upper = face(u, fx, sx, nxt, nf, ns)
                change = [a - b for a, b in zip(upper, lower)]
                pair = pl.multiple_of(p // 2 * 256, 256)
                for d, ghosts, regs, coordinate, shift in ((1, ghost_y, ry, q, 16), (2, ghost_z, rz, r, 1)):
                    gu = [
                        ghosts[pl.ds(pl.multiple_of(sub * 80 + f * 16 + half * 8, 8), 8), pl.ds(pair, 256)]
                        for f in range(5)
                    ]
                    fc, sc = dirflux(u, prims, d)
                    first, last = coordinate == 0, coordinate == 15
                    ul = [jnp.where(first, a, pltpu.roll(b, shift, 1)) for a, b in zip(gu, u)]
                    fl, sl = dirflux(ul, speeds(ul), d)
                    lo = face(ul, fl, sl, u, fc, sc)
                    uh = [jnp.where(last, a, b) for a, b in zip(gu, u)]
                    fh, sh = dirflux(uh, speeds(uh), d)
                    top = face(u, fc, sc, uh, fh, sh)
                    for f in range(5):
                        hi = jnp.where(last, top[f], pltpu.roll(lo[f], 256 - shift, 1))
                        change[f] = change[f] + (hi - lo[f])
                        edge = jnp.where(first, lo[f], jnp.where(last, hi, 0.0))
                        regs[f, rows, pl.ds(pair, 256)] = regs[f, rows, pl.ds(pair, 256)] + edge
                for f in range(5):
                    fu[f, rows, pl.ds(pl.multiple_of((p + 1) * 256, 256), 256)] = u[f] - courant * change[f]
                return nxt, nprims[0], nprims[1], nprims[2], upper

            final = lax.fori_loop(0, BOX, plane, (u0, p0[0], p0[1], p0[2], start))
            for f in range(5):
                rx[f, rows, 256:512] = rx[f, rows, 256:512] + final[4][f]


def fine_results(fu, rx, ry, rz, pa, py, pz, big, stage):
    stage[16 * STAGE_ROWS :, :] = jnp.zeros((STAGE_ROWS, 128), F32)
    tile_lane = lax.broadcasted_iota(jnp.int32, (16, 128), 1)
    left = tile_lane < 64

    def put(line, tile):
        for half in range(2):
            stage[pl.ds(half * 8 * STAGE_ROWS + line, 8, stride=STAGE_ROWS), :] = tile[half * 8 : half * 8 + 8]

    def pooled(pieces, table):
        count = 16 * len(pieces)
        for i, piece in enumerate(pieces):
            put_split(big, i * 16, count, piece)
        return sum_split(dot_nn(big[pl.ds(0, 3 * count), :], table[...]))

    cells = [
        fu[f, :, (2 * x + 1) * 256 : (2 * x + 2) * 256] + fu[f, :, (2 * x + 2) * 256 : (2 * x + 3) * 256]
        for f in range(5)
        for x in range(8)
    ]
    cells += [rx[f, :, s * 256 : s * 256 + 256] for f in range(5) for s in range(2)]
    done = pooled(cells, pa)
    for f in range(5):
        for i in range(4):
            at = (f * 8 + 2 * i) * 16
            put(f * 7 + i, jnp.where(left, done[at : at + 16], done[at + 16 : at + 32]))
        at = (40 + 2 * f) * 16
        put(f * 7 + 4, jnp.where(left, done[at : at + 16], done[at + 16 : at + 32]))
    for line, regs, table, owner in ((5, ry, py, tile_lane % 8), (6, rz, pz, tile_lane // 8 % 8)):
        done = pooled([regs[f, :, x * 256 : x * 256 + 256] for f in range(5) for x in range(8)], table)
        for f in range(5):
            total = done[f * 128 : f * 128 + 16]
            for x in range(1, 8):
                at = (f * 8 + x) * 16
                total = jnp.where(owner == x, done[at : at + 16], total)
            put(f * 7 + line, total)
    for line in range(35, STAGE_ROWS):
        put(line, jnp.zeros((16, 128), F32))


def step_kernel(
    box_lane, lane_box, coarse, keys, fine, ux, uy, uz, pa, py, pz,
    base, fine_new, back, gmax,
    fv, fu, chgf, chgl, pflux, pspeed, exy, cxy, cz, rxy, pay_o, pay_c, arr_o, arr_c,
    hy, hz, gx, gy, gz, tops, mine, g_o, g_c, lhs, ghost_y, ghost_z, rx, ry, rz, big, stage, ret, by_lane, by_box,
    in_sem, out_sem, so, ro, sc, rc, sr, rr, hs, hr, ts, tr,
):
    ix, iy, iz = (lax.axis_index(a) for a in ("gx", "gy", "gz"))
    nx, ny, nz = (lax.axis_size(a) for a in ("gx", "gy", "gz"))
    me = ix * nz + iz
    peers = nx * nz
    load_fine = pltpu.make_async_copy(fine, fv, in_sem.at[0])
    load_fine.start()
    barrier = pltpu.get_barrier_semaphore()

    @pl.loop(1, peers)
    def _(s):
        x, z = plane_peer(s, 1)
        pl.semaphore_signal(barrier, inc=1, device_id=(x, iy, z), device_id_type=MESH)

    @pl.loop(1, ny)
    def _(s):
        pl.semaphore_signal(barrier, inc=1, device_id=(ix, lax.rem(iy + s, ny), iz), device_id_type=MESH)

    exy[...] = onehot(keys[0:1, :], 512)
    pack(coarse, keys[1:2, :], exy, pay_o, cxy, cz, rxy)
    for part in range(8):
        pay_o[pl.ds(part * 8 * OUT_ROWS + 15, 8, stride=OUT_ROWS), :] = jnp.zeros((8, 128), F32)
    pl.semaphore_wait(barrier, peers - 1 + ny - 1)
    old_patch = start_patches(pay_o, arr_o, OUT_ROWS, so, ro)
    arr_o[lanes_of_peer(me, OUT_ROWS), :] = pay_o[lanes_of_peer(me, OUT_ROWS), :]

    best = coarse_changes(coarse, keys[2:3, :], chgf, chgl, pflux, pspeed, hy, hz)
    load_fine.wait()

    def fine_plane(p, best):
        at = pl.multiple_of(p * 256, 256)
        u = [fv[:, f, pl.ds(at, 256)] for f in range(5)]
        for f in range(5):
            fu[f, :, pl.ds(pl.multiple_of(p * 256 + 256, 256), 256)] = u[f]
        return jnp.maximum(best, fastest_of(speeds(u)))

    fine_best = lax.fori_loop(0, BOX, fine_plane, jnp.zeros((16, 256), F32))
    mine[...] = jnp.maximum(best, fold(fine_best))

    def top(s):
        return remote(mine, tops.at[s], ts.at[s], tr.at[s], (ix, lax.rem(iy + s, ny), iz))

    @pl.loop(1, ny)
    def _(s):
        top(s).start()

    pack(chgf, keys[1:2, :], exy, pay_c, cxy, cz, rxy)

    @pl.loop(1, ny)
    def _(s):
        top(s).wait()

    best = mine[...]
    for s in range(1, ny):
        best = jnp.maximum(best, tops[s])
    best = jnp.full((8, 128), jnp.max(best), F32)
    for part in range(8):
        pay_c[pl.ds(part * 8 * OUT_ROWS + 15, 8, stride=OUT_ROWS), :] = best
    new_patch = start_patches(pay_c, arr_c, OUT_ROWS, sc, rc)
    arr_c[lanes_of_peer(me, OUT_ROWS), :] = pay_c[lanes_of_peer(me, OUT_ROWS), :]
    up_x, down_x = lax.rem(ix + 1, nx), lax.rem(ix + nx - 1, nx)
    up_y, down_y = lax.rem(iy + 1, ny), lax.rem(iy + ny - 1, ny)
    up_z, down_z = lax.rem(iz + 1, nz), lax.rem(iz + nz - 1, nz)
    sides = [
        remote(coarse.at[:, coarse.shape[1] - 1], gx.at[0], hs.at[0], hr.at[0], (up_x, iy, iz)),
        remote(coarse.at[:, 0], gx.at[1], hs.at[1], hr.at[1], (down_x, iy, iz)),
        remote(hy.at[1], gy.at[0], hs.at[2], hr.at[2], (ix, up_y, iz)),
        remote(hy.at[0], gy.at[1], hs.at[3], hr.at[3], (ix, down_y, iz)),
        remote(hz.at[1], gz.at[0], hs.at[4], hr.at[4], (ix, iy, up_z)),
        remote(hz.at[0], gz.at[1], hs.at[5], hr.at[5], (ix, iy, down_z)),
    ]
    for side in sides:
        side.start()

    @pl.loop(1, peers)
    def _(s):
        old_patch(s).wait()

    @pl.loop(1, peers)
    def _(s):
        new_patch(s).wait()

    for part in range(8):
        best = jnp.maximum(best, arr_c[pl.ds(part * 8 * OUT_ROWS + 15, 8, stride=OUT_ROWS), :])
    gmax[...] = best
    courant = COURANT_NUMBER / jnp.max(best)
    for arr, g in ((arr_o, g_o), (arr_c, g_c)):
        for lane in range(64):
            by_lane[lane] = arr[lane * OUT_ROWS : (lane + 1) * OUT_ROWS, :]
        for b in range(16):
            g[pl.ds(b, OUT_ROWS, stride=16), :] = by_lane[box_lane[b]]
    fine_steps(courant, g_o, g_c, ux, uy, uz, fu, lhs, ghost_y, ghost_z, rx, ry, rz)
    fine_results(fu, rx, ry, rz, pa, py, pz, big, stage)
    for b in range(17):
        by_box[b] = stage[b * STAGE_ROWS : (b + 1) * STAGE_ROWS, :]
    for lane in range(64):
        ret[lane * BACK_ROWS : (lane + 1) * BACK_ROWS, :] = by_box[lane_box[lane]][:BACK_ROWS]
    back_patch = start_patches(ret, back, BACK_ROWS, sr, rr)
    own = pltpu.make_async_copy(
        ret.at[lanes_of_peer(me, BACK_ROWS), :], back.at[lanes_of_peer(me, BACK_ROWS), :], out_sem.at[0]
    )
    own.start()
    for f in range(5):
        for p in range(16):
            fv[:, f, p * 256 : p * 256 + 256] = fu[f, :, (p + 1) * 256 : (p + 2) * 256]
    store_fine = pltpu.make_async_copy(fv, fine_new, out_sem.at[1])
    store_fine.start()
    for side in sides:
        side.wait()
    coarse_base(coarse, chgl, courant, gx, gy, gz, hy, hz)
    store_base = pltpu.make_async_copy(chgl, base, out_sem.at[2])
    store_base.start()
    own.wait()
    store_fine.wait()
    store_base.wait()

    @pl.loop(1, peers)
    def _(s):
        back_patch(s).wait()


def apply_kernel(base, keys, arr, gmax, out, lxy, lz, dxy, dz):
    nx, _, nz = base.shape[1:]
    courant = COURANT_NUMBER / jnp.max(gmax[...])
    left = lax.broadcasted_iota(jnp.int32, (16, 128), 1) < 64
    left64 = lax.broadcasted_iota(jnp.int32, (64, 128), 1) < 64

    def lanes_of(line):
        return jnp.concatenate(
            [arr[pl.ds(part * 8 * BACK_ROWS + line, 8, stride=BACK_ROWS), :] for part in range(8)], axis=0
        )

    flat = [(f, i) for f in range(5) for i in range(6)]
    for first in range(0, 30, 2):
        pair = flat[first : first + 2]
        turned = jnp.concatenate([lanes_of(f * 7 + i) for f, i in pair], axis=0).T
        for second in range(2):
            pieces = []
            for couple in range(4):
                even = jnp.concatenate(
                    [turned[a * 64 + couple * 16 : a * 64 + couple * 16 + 8] for a in range(2)], axis=0
                )
                odd = jnp.concatenate(
                    [turned[a * 64 + couple * 16 + 8 : a * 64 + couple * 16 + 16] for a in range(2)], axis=0
                )
                if second == 0:
                    pieces.append(jnp.where(left, even, pltpu.roll(odd, 64, 1)))
                else:
                    pieces.append(jnp.where(left, pltpu.roll(even, 64, 1), odd))
            put_split(lxy, (first + second) * 16, 480, jnp.concatenate(pieces, axis=1))
    for f in range(5):
        both = jnp.concatenate([lanes_of(f * 7 + 6), lanes_of(f * 7 + 6)], axis=0).T
        put_split(lz, f * 64, 320, jnp.where(left64, both[:64], both[64:]))
    dxy[...] = sum_split(dot_nn(lxy[...], onehot(keys[0:1, :], 512)))
    dz[...] = sum_split(dot_nn(lz[...], onehot(keys[1:2, :], 128)))

    spot = lax.broadcasted_iota(jnp.int32, (CORE, nz), 1) % BOX
    refined = jnp.broadcast_to(keys[2:3, :], (CORE, nz)) >= 0
    inside = refined & (spot >= SHIFT) & (spot < SHIFT + CORE)
    z_sign = courant * jnp.where(spot == SHIFT - 1, -1.0, jnp.where(spot == SHIFT + CORE, 1.0, 0.0))
    mid = slice(SHIFT, SHIFT + CORE)
    for f in range(5):
        for x in range(nx):
            out[f, x] = base[f, x]
        for side, x, sign in ((0, SHIFT - 1, -1.0), (1, SHIFT + CORE, 1.0)):
            at = (f * 6 + 4) * 16 + side * 8
            out[f, x, mid, :] = out[f, x, mid, :] + (sign * courant) * dxy[at : at + 8, :]
            at = (f * 6 + 5) * 16 + side * 8
            for i in range(CORE):
                y = x
                out[f, SHIFT + i, y : y + 1, :] = (
                    out[f, SHIFT + i, y : y + 1, :] + (sign * courant) * dxy[at + i : at + i + 1, :]
                )
        for i in range(CORE):
            fixed = out[f, SHIFT + i, mid, :] + z_sign * dz[f * 64 + i * 8 : f * 64 + i * 8 + 8, :]
            average = dxy[f * 96 + i * 8 : f * 96 + i * 8 + 8, :]
            out[f, SHIFT + i, mid, :] = jnp.where(inside, average, fixed)


VMEM = pl.BlockSpec(memory_space=pltpu.VMEM)
SMEM = pl.BlockSpec(memory_space=pltpu.SMEM)
ANY = pl.BlockSpec(memory_space=pl.ANY)


def shape(*dims):
    return jax.ShapeDtypeStruct(dims, F32)


def step_call(box_lane, lane_box, coarse, keys, fine):
    peers = lax.axis_size("gx") * lax.axis_size("gz")
    count_y = lax.axis_size("gy")
    _, nx, ny, nz = coarse.shape
    dma = pltpu.SemaphoreType.DMA
    tables = fine_tables()

    def vmem(*dims, dtype=F32):
        return pltpu.VMEM(dims, dtype)

    return pl.pallas_call(
        step_kernel,
        out_shape=[shape(*coarse.shape), shape(*fine.shape), shape(64 * BACK_ROWS, 128), shape(8, 128)],
        in_specs=[SMEM, SMEM, VMEM, VMEM, ANY] + [VMEM] * 6,
        out_specs=[ANY, ANY, ANY, VMEM],
        scratch_shapes=[
            vmem(*fine.shape),
            vmem(5, 16, 18 * 256),
            vmem(5, nx, ny, nz),
            vmem(5, nx, ny, nz),
            vmem(5, ny, nz),
            vmem(ny, nz),
            vmem(512, nz, dtype=BF16),
            vmem(480, nz, dtype=BF16),
            vmem(960, nz, dtype=BF16),
            vmem(160, 512),
            *[vmem(64 * OUT_ROWS, 128)] * 4,
            vmem(2, 5, nx, nz),
            vmem(2, 5, ny, 128),
            vmem(2, 5, ny, nz),
            vmem(2, 5, nx, nz),
            vmem(2, 5, ny, 128),
            vmem(count_y, 8, 128),
            vmem(8, 128),
            vmem(16 * OUT_ROWS, 128),
            vmem(16 * OUT_ROWS, 128),
            vmem(480, 128, dtype=BF16),
            vmem(160, 2048),
            vmem(160, 2048),
            vmem(5, 16, 512),
            vmem(5, 16, 2048),
            vmem(5, 16, 2048),
            vmem(2400, 256, dtype=BF16),
            vmem(17 * STAGE_ROWS, 128),
            vmem(64 * BACK_ROWS, 128),
            vmem(64, OUT_ROWS, 128),
            vmem(17, STAGE_ROWS, 128),
            dma((1,)),
            dma((3,)),
            *[dma((peers,))] * 6,
            dma((6,)),
            dma((6,)),
            dma((count_y,)),
            dma((count_y,)),
        ],
        compiler_params=pltpu.CompilerParams(
            collective_id=0, has_side_effects=True, vmem_limit_bytes=VMEM_LIMIT
        ),
        name="step",
    )(box_lane, lane_box, coarse, keys, fine, *tables)


def apply_call(base, keys, arr, gmax):
    nz = base.shape[3]
    return pl.pallas_call(
        apply_kernel,
        out_shape=shape(*base.shape),
        in_specs=[VMEM] * 4,
        out_specs=VMEM,
        scratch_shapes=[
            pltpu.VMEM((1440, 512), BF16),
            pltpu.VMEM((960, 128), BF16),
            pltpu.VMEM((480, nz), F32),
            pltpu.VMEM((320, nz), F32),
        ],
        compiler_params=pltpu.CompilerParams(vmem_limit_bytes=VMEM_LIMIT),
        name="reflux_apply",
    )(base, keys, arr, gmax)


def tables_of(slot_owner, box_corner, count_gz):
    owners = slot_owner.reshape(-1)
    slots = owners.shape[0]
    index = jnp.arange(slots, dtype=jnp.int32)
    rank = jnp.sum(
        (owners[:, None] == owners[None, :]) & (index[None, :] < index[:, None]), axis=1, dtype=jnp.int32
    )
    slot_lane = jnp.where(owners >= 0, owners * 2 + rank, -1)
    lane_z = jnp.repeat(slot_lane, BOX)
    spot = jnp.arange(slots * BOX, dtype=jnp.int32) % BOX
    on = lane_z >= 0
    inner = on & (spot >= SHIFT) & (spot < SHIFT + CORE)
    outer = on & ((spot == SHIFT - 1) | (spot == SHIFT + CORE))
    key_xy = jnp.where(inner, (spot - SHIFT) * 64 + lane_z, -1)
    key_z = jnp.where(outer, jnp.where(spot < SHIFT, 0, 64) + lane_z, -1)
    keys = jnp.stack([key_xy, key_z, lane_z] + [lane_z] * 5)
    source = box_corner[:, 0] * count_gz + box_corner[:, 2] // slots
    number = jnp.arange(source.shape[0], dtype=jnp.int32)
    place = jnp.sum(
        (source[:, None] == source[None, :]) & (number[None, :] < number[:, None]), axis=1, dtype=jnp.int32
    )
    box_lane = source * 2 + place
    lanes = jnp.arange(64, dtype=jnp.int32)
    lane_box = jnp.min(jnp.where(box_lane[None, :] == lanes[:, None], number[None, :], 16), axis=1)
    return keys, box_lane, lane_box


def local(coarse_old, fine_old, slot_owner, box_corner):
    keys, box_lane, lane_box = tables_of(slot_owner, box_corner, lax.axis_size("gz"))
    base, fine_new, back, gmax = step_call(box_lane, lane_box, coarse_old, keys, fine_old)
    coarse_new = apply_call(base, keys, back, gmax)
    return (coarse_new, fine_new)


def solution(mesh):
    in_specs = (
        P(None, "gx", "gy", "gz"),
        P(("gx", "gy", "gz"), None, None),
        P("gx", "gy", "gz"),
        P(("gx", "gy", "gz"), None),
    )
    out_specs = (P(None, "gx", "gy", "gz"), P(("gx", "gy", "gz"), None, None))
    return jax.shard_map(local, mesh=mesh, in_specs=in_specs, out_specs=out_specs, check_vma=False)
```

time: 131 us -> 105 us (0.80)
  Pallas kernels: 119 us -> 93.4 us
    pallas_call x5 -> x2, Pallas kernels: 119 us -> 93.4 us  [the longest x1 87.8 us: step_call(): pl.pallas_call(step_kernel, out_shape=[shape(*coarse.shape), shape(*fine....]
    unnamed x4 -> x6, local copies, waits for them, and re-layouts: 5.27 us -> 5.27 us
where the time goes in v2:
time: 105 us
  Pallas kernels  93.4 us (89%)
  local copies, waits for them, and re-layouts  6.06 us (6%)
  other arithmetic  4.69 us (4%)
    pallas_call x1, Pallas kernels, step_call(): pl.pallas_call(step_kernel, out_shape=[shape(*coarse.shape), shape(*fine....  87.8 us
    pallas_call x1, Pallas kernels, apply_call(): pl.pallas_call(apply_kernel, out_shape=shape(*base.shape), in_specs=[VMEM...  5.62 us
    unnamed x6, local copies, waits for them, and re-layouts  5.27 us

profile of v2, /device:TPU:4, one launch (start us, length us, event | category | flops | bytes accessed | tf_op | source)
XLA Modules:
  0.0 104.9 jit_solution(14469158783554831228)
XLA Ops:
  0.6 0.9 convert_reduce_fusion
  1.5 0.7 compare_select_fusion.1
  2.2 0.8 bitcast_add_fusion
  3.0 0.8 add_bitcast_fusion
  3.7 0.2 convert_reduce_fusion.1
  3.9 0.8 multiply_add_fusion.box_lane
  4.7 0.0 copy-start.1
  4.7 0.6 select_reduce_fusion.lane_box
  5.3 0.1 broadcast_in_dim.40
  5.4 0.1 reshape.162
  5.5 0.6 stack.2.keys
  6.1 3.4 %copy.16.fine = f32[16,5,4096]{2,1,0:T(8,128)} copy(f32[16,5,4096]{2,0,1:T(8,128)} %param.11) | data formatting | bytes 2621440 | tf_op args[1]
  9.6 0.0 copy-done.1
  9.6 87.8 %step.1 = (f32[5,16,16,512]{3,2,1,0:T(8,128)}, f32[16,5,4096]{2,1,0:T(8,128)}, f32[2304,128]{1,0:T(8,128)}, f32[8,128]{1,0:T(8,128)}) custom-call(s32[16]{0:T(128)} %copy-done.1, s32[64]{0:T(128)} %select_reduce_fusion.lane_box, f32[5,16,16,512]{3,2,1,0:T(8,128)} %coarse.1, s32[8,512]{1,0:T(8,128)} %stack.2.keys, f32[16,5,4096]{2,1,0:T(8,128)} %copy.16.fine, ...), custom_call_target="tpu_custom_call" | custom-call | tf_op jit(solution)/shard_map/step/pallas_call | solution.py:644
  97.4 0.0 copy-start
  97.4 5.6 %reflux_apply.1 = f32[5,16,16,512]{3,2,1,0:T(8,128)} custom-call(f32[5,16,16,512]{3,2,1,0:T(8,128)} %get-tuple-element.6.base, s32[8,512]{1,0:T(8,128)} %stack.2.keys, f32[2304,128]{1,0:T(8,128)} %get-tuple-element.7.arr, f32[8,128]{1,0:T(8,128)} %get-tuple-element.8.gmax), custom_call_target="tpu_custom_call" | custom-call | tf_op jit(solution)/shard_map/reflux_apply/pallas_call | solution.py:698
  103.0 0.0 copy-done
  103.0 1.8 %copy.17 = f32[16,5,4096]{2,0,1:T(8,128)} copy(f32[16,5,4096]{2,1,0:T(8,128)S(1)} %copy-done) | data formatting | bytes 2621440
  (1 shorter events, 0.0 us)
Async XLA Ops:
  4.7 4.9 %copy-start.1 = (s32[16]{0:T(128)}, s32[16]{0:T(128)S(1)}, u32[]{:S(2)}) copy-start(s32[16]{0:T(128)S(1)} %multiply_add_fusion.box_lane) | copy-start | bytes 196
  97.4 5.6 %copy-start = (f32[16,5,4096]{2,1,0:T(8,128)S(1)}, f32[16,5,4096]{2,1,0:T(8,128)}, u32[]{:S(2)}) copy-start(f32[16,5,4096]{2,1,0:T(8,128)} %get-tuple-element.15) | copy-start | bytes 3932164

commit v3 on v2

--- a/solution.py
+++ b/solution.py
@@ -1,8 +1,5 @@
-import functools
-
 import jax
 import jax.numpy as jnp
-import numpy as np
 from jax import lax
 from jax.experimental import pallas as pl
 from jax.experimental.pallas import tpu as pltpu
@@ -91,44 +88,6 @@
 def onehot(key_row, rows):
     index = lax.broadcasted_iota(jnp.int32, (rows, key_row.shape[1]), 0)
     return jnp.where(index == key_row, 1.0, 0.0).astype(BF16)
-
-
-def fine_tables():
-    c = np.arange(128)
-    side, high, low = c // 64, c // 8 % 8, c % 8
-    q, r = np.arange(256) // 16, np.arange(256) % 16
-    half_q, half_r = q // 2, r // 2
-    edge_q = np.where(q == 0, 0, np.where(q == 15, 1, -1))
-    edge_r = np.where(r == 0, 0, np.where(r == 15, 1, -1))
-
-    def both(*conditions):
-        return np.logical_and.reduce(np.broadcast_arrays(*conditions))
-
-    up_x = np.concatenate(
-        [
-            both(side[:, None] == s, low[:, None] == half_q[None], high[:, None] == half_r[None])
-            for s in range(2)
-        ],
-        axis=1,
-    )
-    up_y = np.concatenate(
-        [
-            both(low[:, None] == x, side[:, None] == edge_q[None], high[:, None] == half_r[None])
-            for x in range(8)
-        ],
-        axis=1,
-    )
-    up_z = np.concatenate(
-        [
-            both(high[:, None] == x, side[:, None] == edge_r[None], low[:, None] == half_q[None])
-            for x in range(8)
-        ],
-        axis=1,
-    )
-    pool_a = both(half_q[:, None] == low[None], half_r[:, None] == high[None]) * 0.125
-    pool_y = both(edge_q[:, None] == side[None], half_r[:, None] == high[None]) * 0.125
-    pool_z = both(edge_r[:, None] == side[None], half_q[:, None] == low[None]) * 0.125
-    return [jnp.asarray(t.astype(np.float32), BF16) for t in (up_x, up_y, up_z, pool_a, pool_y, pool_z)]
 
 
 def plane_peer(s, sign):
@@ -320,135 +279,219 @@
             chgl[f, x, :, nz - 128 :] = chgl[f, x, :, nz - 128 :] - jnp.where(tile == 127, add, 0.0)
 
 
-def fine_steps(courant, g_o, g_c, ux, uy, uz, fu, lhs, ghost_y, ghost_z, rx, ry, rz):
-    rx[...] = jnp.zeros_like(rx)
-    ry[...] = jnp.zeros_like(ry)
-    rz[...] = jnp.zeros_like(rz)
-
-    def ghost(part, table):
+def spread_table():
+    cell = lax.broadcasted_iota(jnp.int32, (128, 512), 0)
+    lane = lax.broadcasted_iota(jnp.int32, (128, 512), 1)
+    wanted = (lane >> 8) * 64 + ((lane & 15) >> 1) * 8 + ((lane >> 5) & 7)
+    return jnp.where(cell == wanted, 1.0, 0.0).astype(BF16)
+
+
+def pool_table():
+    lane = lax.broadcasted_iota(jnp.int32, (256, 128), 0)
+    cell = lax.broadcasted_iota(jnp.int32, (256, 128), 1) & 63
+    wanted = ((lane & 15) >> 1) * 8 + ((lane >> 5) & 7)
+    return jnp.where(cell == wanted, 0.125, 0.0).astype(BF16)
+
+
+def plane_lanes(p):
+    return pl.ds(pl.multiple_of(p * 256, 256), 256)
+
+
+def fine_inner(fu, chg, edge_y, edge_z):
+    lane = lax.broadcasted_iota(jnp.int32, (8, 256), 1)
+    inner_y = jnp.where(lane >= 16, 1.0, 0.0)
+    inner_z = jnp.where(lane & 15 != 0, 1.0, 0.0)
+    tile = lax.broadcasted_iota(jnp.int32, (8, 128), 1)
+
+    @pl.loop(0, 2)
+    def _(half):
+        rows = pl.ds(pl.multiple_of(half * 8, 8), 8)
+
+        def load(p):
+            return [fu[f, rows, plane_lanes(p)] for f in range(5)]
+
+        def plane(p, carry):
+            u, velocity, pressure, sound, lower = carry
+            prims = (velocity, pressure, sound)
+            after = load(jnp.minimum(p + 1, BOX - 1))
+            next_prims = speeds(after)
+            flux, speed = dirflux(u, prims, 0)
+            next_flux, next_speed = dirflux(after, next_prims, 0)
+            more = jnp.where(p < BOX - 1, 1.0, 0.0)
+            upper = [piece * more for piece in face(u, flux, speed, after, next_flux, next_speed)]
+            change = [a - b for a, b in zip(upper, lower)]
+            for d, shift, keep in ((1, 16, inner_y), (2, 1, inner_z)):
+                flux, speed = dirflux(u, prims, d)
+                ru = [pltpu.roll(piece, shift, 1) for piece in u]
+                rf = [ru[1 + d]] + [pltpu.roll(piece, shift, 1) for piece in flux[1:]]
+                low = face(ru, rf, pltpu.roll(speed, shift, 1), u, flux, speed)
+                low = [piece * keep for piece in low]
+                change = [c + (pltpu.roll(b, 256 - shift, 1) - b) for c, b in zip(change, low)]
+            seat = lax.rem(p, 8)
+            at = pl.multiple_of(p // 8 * 128, 128)
+            here_y = tile >> 4 == seat
+            here_z = tile & 15 == p
+            for f in range(5):
+                chg[f, rows, plane_lanes(p)] = change[f]
+                for side, shift in ((0, seat * 16), (1, lax.rem(seat * 16 + 16, 128))):
+                    moved = pltpu.roll(u[f][:, side * 128 : side * 128 + 128], shift, 1)
+                    place = pl.ds(side * 256 + at, 128)
+                    edge_y[f, rows, place] = jnp.where(here_y, moved, edge_y[f, rows, place])
+                for side, shift in ((0, p), (1, lax.rem(p + 113, 128))):
+                    for t in range(2):
+                        moved = pltpu.roll(u[f][:, t * 128 : t * 128 + 128], shift, 1)
+                        place = slice(side * 256 + t * 128, side * 256 + t * 128 + 128)
+                        edge_z[f, rows, place] = jnp.where(here_z, moved, edge_z[f, rows, place])
+            return after, next_prims[0], next_prims[1], next_prims[2], upper
+
+        first = load(0)
+        prims = speeds(first)
+        nothing = [jnp.zeros((8, 256), F32)] * 5
+        lax.fori_loop(0, BOX, plane, (first, prims[0], prims[1], prims[2], nothing))
+
+
+def fine_outer(sub, fu, chg, edge_y, edge_z, ghosts, regs):
+    last = (BOX - 1) * 256
+    for part in range(3):
+        for side in range(2):
+            lanes = slice(side * 256, side * 256 + 256)
+            if part == 0:
+                inside = [fu[f, :, side * last : side * last + 256] for f in range(5)]
+            else:
+                inside = [(edge_y, edge_z)[part - 1][f, :, lanes] for f in range(5)]
+            at = part * 160 + sub * 80
+            outside = [ghosts[at + f * 16 : at + f * 16 + 16, lanes] for f in range(5)]
+            lower, upper = (outside, inside) if side == 0 else (inside, outside)
+            fl, sl = dirflux(lower, speeds(lower), part)
+            fh, sh = dirflux(upper, speeds(upper), part)
+            through = face(lower, fl, sl, upper, fh, sh)
+            for f in range(5):
+                line = (part * 5 + f) * 16
+                if sub == 0:
+                    regs[line : line + 16, lanes] = through[f]
+                else:
+                    regs[line : line + 16, lanes] = regs[line : line + 16, lanes] + through[f]
+                if part == 0:
+                    place = slice(side * last, side * last + 256)
+                    chg[f, :, place] = chg[f, :, place] + (through[f] if side else -through[f])
+                else:
+                    (edge_y, edge_z)[part - 1][f, :, lanes] = through[f] if side else -through[f]
+
+
+def fine_update(courant, fu, chg, edge_y, edge_z):
+    tile = lax.broadcasted_iota(jnp.int32, (16, 128), 1)
+    y_side = (tile < 16, tile >= 112)
+    z_side = (tile & 15 == 0, tile & 15 == 15)
+
+    @pl.loop(0, BOX)
+    def _(p):
+        seat = lax.rem(p, 8)
+        at = pl.multiple_of(p // 8 * 128, 128)
+        y_shift = (lax.rem(128 - seat * 16, 128), 112 - seat * 16)
+        z_shift = (lax.rem(128 - p, 128), 15 - p)
         for f in range(5):
-            old = g_o[pl.ds((f * 3 + part) * 16, 16), :]
-            change = g_c[pl.ds((f * 3 + part) * 16, 16), :]
-            put_split(lhs, f * 16, 160, old)
-            put_split(lhs, 80 + f * 16, 160, 0.5 * (old + (old - courant * change)))
-        return sum_split(dot_nn(lhs[...], table[...]))
-
-    ghost_y[...] = ghost(1, uy)
-    ghost_z[...] = ghost(2, uz)
-    ghost_x = ghost(0, ux)
-    lane = lax.broadcasted_iota(jnp.int32, (8, 256), 1)
-    q, r = lane // 16, lane % 16
-    for sub in range(2):
+            for t in range(2):
+                place = pl.ds(pl.multiple_of(p * 256 + t * 128, 128), 128)
+                change = chg[f, :, place]
+                moved = pltpu.roll(edge_y[f, :, pl.ds(t * 256 + at, 128)], y_shift[t], 1)
+                change = change + jnp.where(y_side[t], moved, 0.0)
+                for side in range(2):
+                    piece = edge_z[f, :, side * 256 + t * 128 : side * 256 + t * 128 + 128]
+                    change = change + jnp.where(z_side[side], pltpu.roll(piece, z_shift[side], 1), 0.0)
+                fu[f, :, place] = fu[f, :, place] - courant * change
+
+
+def fine_ghosts(courant, g_o, g_c, spread, lhs):
+    for part in range(3):
         for f in range(5):
-            fu[f, :, 0:256] = ghost_x[sub * 80 + f * 16 : sub * 80 + f * 16 + 16, :256]
-            fu[f, :, 17 * 256 :] = ghost_x[sub * 80 + f * 16 : sub * 80 + f * 16 + 16, 256:]
-
-        @pl.loop(0, 2)
-        def _(half):
-            rows = pl.ds(pl.multiple_of(half * 8, 8), 8)
-
-            def load(p):
-                return [fu[f, rows, pl.ds(pl.multiple_of(p * 256, 256), 256)] for f in range(5)]
-
-            ghost_u = load(0)
-            gp = speeds(ghost_u)
-            gf, gs = dirflux(ghost_u, gp, 0)
-            u0 = load(1)
-            p0 = speeds(u0)
-            f0, s0 = dirflux(u0, p0, 0)
-            start = face(ghost_u, gf, gs, u0, f0, s0)
-            for f in range(5):
-                rx[f, rows, 0:256] = rx[f, rows, 0:256] + start[f]
-
-            def plane(p, carry):
-                u, vel, pressure, sound, lower = carry
-                prims = (vel, pressure, sound)
-                nxt = load(p + 2)
-                nprims = speeds(nxt)
-                fx, sx = dirflux(u, prims, 0)
-                nf, ns = dirflux(nxt, nprims, 0)
-                upper = face(u, fx, sx, nxt, nf, ns)
-                change = [a - b for a, b in zip(upper, lower)]
-                pair = pl.multiple_of(p // 2 * 256, 256)
-                for d, ghosts, regs, coordinate, shift in ((1, ghost_y, ry, q, 16), (2, ghost_z, rz, r, 1)):
-                    gu = [
-                        ghosts[pl.ds(pl.multiple_of(sub * 80 + f * 16 + half * 8, 8), 8), pl.ds(pair, 256)]
-                        for f in range(5)
-                    ]
-                    fc, sc = dirflux(u, prims, d)
-                    first, last = coordinate == 0, coordinate == 15
-                    ul = [jnp.where(first, a, pltpu.roll(b, shift, 1)) for a, b in zip(gu, u)]
-                    fl, sl = dirflux(ul, speeds(ul), d)
-                    lo = face(ul, fl, sl, u, fc, sc)
-                    uh = [jnp.where(last, a, b) for a, b in zip(gu, u)]
-                    fh, sh = dirflux(uh, speeds(uh), d)
-                    top = face(u, fc, sc, uh, fh, sh)
-                    for f in range(5):
-                        hi = jnp.where(last, top[f], pltpu.roll(lo[f], 256 - shift, 1))
-                        change[f] = change[f] + (hi - lo[f])
-                        edge = jnp.where(first, lo[f], jnp.where(last, hi, 0.0))
-                        regs[f, rows, pl.ds(pair, 256)] = regs[f, rows, pl.ds(pair, 256)] + edge
-                for f in range(5):
-                    fu[f, rows, pl.ds(pl.multiple_of((p + 1) * 256, 256), 256)] = u[f] - courant * change[f]
-                return nxt, nprims[0], nprims[1], nprims[2], upper
-
-            final = lax.fori_loop(0, BOX, plane, (u0, p0[0], p0[1], p0[2], start))
-            for f in range(5):
-                rx[f, rows, 256:512] = rx[f, rows, 256:512] + final[4][f]
-
-
-def fine_results(fu, rx, ry, rz, pa, py, pz, big, stage):
+            old = g_o[(f * 3 + part) * 16 : (f * 3 + part) * 16 + 16, :]
+            change = g_c[(f * 3 + part) * 16 : (f * 3 + part) * 16 + 16, :]
+            put_split(lhs, part * 160 + f * 16, 480, old)
+            put_split(lhs, part * 160 + 80 + f * 16, 480, 0.5 * (old + (old - courant * change)))
+    return sum_split(dot_nn(lhs[...], spread[...]))
+
+
+def fine_results(fu, regs, pool, big, stage):
     stage[16 * STAGE_ROWS :, :] = jnp.zeros((STAGE_ROWS, 128), F32)
-    tile_lane = lax.broadcasted_iota(jnp.int32, (16, 128), 1)
-    left = tile_lane < 64
-
-    def put(line, tile):
+    left = lax.broadcasted_iota(jnp.int32, (16, 128), 1) < 64
+    count = 16 * 70
+    for f in range(5):
+        for x in range(8):
+            at = x * 512
+            put_split(big, (f * 8 + x) * 16, count, fu[f, :, at : at + 256] + fu[f, :, at + 256 : at + 512])
+    for line in range(15):
+        for side in range(2):
+            piece = regs[line * 16 : line * 16 + 16, side * 256 : side * 256 + 256]
+            put_split(big, (40 + line * 2 + side) * 16, count, piece)
+    done = sum_split(dot_nn(big[...], pool[...]))
+
+    def put(line, group):
+        tile = jnp.where(left, done[group * 16 : group * 16 + 16], done[group * 16 + 16 : group * 16 + 32])
         for half in range(2):
             stage[pl.ds(half * 8 * STAGE_ROWS + line, 8, stride=STAGE_ROWS), :] = tile[half * 8 : half * 8 + 8]
 
-    def pooled(pieces, table):
-        count = 16 * len(pieces)
-        for i, piece in enumerate(pieces):
-            put_split(big, i * 16, count, piece)
-        return sum_split(dot_nn(big[pl.ds(0, 3 * count), :], table[...]))
-
-    cells = [
-        fu[f, :, (2 * x + 1) * 256 : (2 * x + 2) * 256] + fu[f, :, (2 * x + 2) * 256 : (2 * x + 3) * 256]
-        for f in range(5)
-        for x in range(8)
-    ]
-    cells += [rx[f, :, s * 256 : s * 256 + 256] for f in range(5) for s in range(2)]
-    done = pooled(cells, pa)
     for f in range(5):
         for i in range(4):
-            at = (f * 8 + 2 * i) * 16
-            put(f * 7 + i, jnp.where(left, done[at : at + 16], done[at + 16 : at + 32]))
-        at = (40 + 2 * f) * 16
-        put(f * 7 + 4, jnp.where(left, done[at : at + 16], done[at + 16 : at + 32]))
-    for line, regs, table, owner in ((5, ry, py, tile_lane % 8), (6, rz, pz, tile_lane // 8 % 8)):
-        done = pooled([regs[f, :, x * 256 : x * 256 + 256] for f in range(5) for x in range(8)], table)
-        for f in range(5):
-            total = done[f * 128 : f * 128 + 16]
-            for x in range(1, 8):
-                at = (f * 8 + x) * 16
-                total = jnp.where(owner == x, done[at : at + 16], total)
-            put(f * 7 + line, total)
+            put(f * 7 + i, f * 8 + 2 * i)
+        for part in range(3):
+            put(f * 7 + 4 + part, 40 + (part * 5 + f) * 2)
     for line in range(35, STAGE_ROWS):
-        put(line, jnp.zeros((16, 128), F32))
+        for half in range(2):
+            stage[pl.ds(half * 8 * STAGE_ROWS + line, 8, stride=STAGE_ROWS), :] = jnp.zeros((8, 128), F32)
+
+
+def candidate_keys(owner, keys):
+    slots = owner.shape[0]
+    lane = lax.broadcasted_iota(jnp.int32, (8, slots * BOX), 1)
+    slot = lane >> 4
+    spot = lane & 15
+    owners = jnp.full(lane.shape, -1, jnp.int32)
+    for k in range(slots):
+        owners = jnp.where(slot == k, owner[k], owners)
+    rank = jnp.zeros(lane.shape, jnp.int32)
+    for k in range(slots - 1):
+        rank = rank + jnp.where((owners == owner[k]) & (slot > k), 1, 0)
+    seat = jnp.where(owners >= 0, owners * 2 + rank, -1)
+    on = seat >= 0
+    inner = on & (spot >= SHIFT) & (spot < SHIFT + CORE)
+    keys[0:1, :] = jnp.where(inner, (spot - SHIFT) * 64 + seat, -1)[0:1]
+    outer = jnp.where(spot == SHIFT - 1, seat, jnp.where(spot == SHIFT + CORE, seat + 64, -1))
+    keys[1:2, :] = jnp.where(on, outer, -1)[0:1]
+    keys[2:8, :] = seat[0:6]
+
+
+def box_tables(corner, slots, count_z, box_lane, lane_box):
+    count = corner.shape[1]
+    sources = [corner[0, b] * count_z + lax.div(corner[2, b], slots) for b in range(count)]
+    lanes = []
+    for b in range(count):
+        place = jnp.int32(0)
+        for i in range(b):
+            place = place + jnp.where(sources[i] == sources[b], 1, 0)
+        lanes.append(sources[b] * 2 + place)
+        box_lane[b] = lanes[b]
+
+    @pl.loop(0, 64)
+    def _(lane):
+        box = jnp.int32(count)
+        for b in range(count):
+            box = jnp.where(box_lane[b] == lane, b, box)
+        lane_box[lane] = box
 
 
 def step_kernel(
-    box_lane, lane_box, coarse, keys, fine, ux, uy, uz, pa, py, pz,
-    base, fine_new, back, gmax,
-    fv, fu, chgf, chgl, pflux, pspeed, exy, cxy, cz, rxy, pay_o, pay_c, arr_o, arr_c,
-    hy, hz, gx, gy, gz, tops, mine, g_o, g_c, lhs, ghost_y, ghost_z, rx, ry, rz, big, stage, ret, by_lane, by_box,
+    owner, corner, coarse, fine,
+    base, fine_new, back, gmax, keys,
+    fu, chg, chgf, chgl, pflux, pspeed, exy, cxy, cz, rxy, pay_o, pay_c, arr_o, arr_c,
+    hy, hz, gx, gy, gz, tops, mine, g_o, g_c, spread, pool, lhs, ghosts, edge_y, edge_z, regs, big, stage,
+    ret, by_lane, by_box, box_lane, lane_box,
     in_sem, out_sem, so, ro, sc, rc, sr, rr, hs, hr, ts, tr,
 ):
     ix, iy, iz = (lax.axis_index(a) for a in ("gx", "gy", "gz"))
     nx, ny, nz = (lax.axis_size(a) for a in ("gx", "gy", "gz"))
     me = ix * nz + iz
     peers = nx * nz
-    load_fine = pltpu.make_async_copy(fine, fv, in_sem.at[0])
+    load_fine = pltpu.make_async_copy(fine, fu, in_sem.at[0])
     load_fine.start()
     barrier = pltpu.get_barrier_semaphore()
 
@@ -461,6 +504,7 @@
     def _(s):
         pl.semaphore_signal(barrier, inc=1, device_id=(ix, lax.rem(iy + s, ny), iz), device_id_type=MESH)
 
+    candidate_keys(owner, keys)
     exy[...] = onehot(keys[0:1, :], 512)
     pack(coarse, keys[1:2, :], exy, pay_o, cxy, cz, rxy)
     for part in range(8):
@@ -473,10 +517,7 @@
     load_fine.wait()
 
     def fine_plane(p, best):
-        at = pl.multiple_of(p * 256, 256)
-        u = [fv[:, f, pl.ds(at, 256)] for f in range(5)]
-        for f in range(5):
-            fu[f, :, pl.ds(pl.multiple_of(p * 256 + 256, 256), 256)] = u[f]
+        u = [fu[f, :, plane_lanes(p)] for f in range(5)]
         return jnp.maximum(best, fastest_of(speeds(u)))
 
     fine_best = lax.fori_loop(0, BOX, fine_plane, jnp.zeros((16, 256), F32))
@@ -517,6 +558,11 @@
     for side in sides:
         side.start()
 
+    fine_inner(fu, chg, edge_y, edge_z)
+    box_tables(corner, owner.shape[0], nz, box_lane, lane_box)
+    spread[...] = spread_table()
+    pool[...] = pool_table()
+
     @pl.loop(1, peers)
     def _(s):
         old_patch(s).wait()
@@ -534,8 +580,13 @@
             by_lane[lane] = arr[lane * OUT_ROWS : (lane + 1) * OUT_ROWS, :]
         for b in range(16):
             g[pl.ds(b, OUT_ROWS, stride=16), :] = by_lane[box_lane[b]]
-    fine_steps(courant, g_o, g_c, ux, uy, uz, fu, lhs, ghost_y, ghost_z, rx, ry, rz)
-    fine_results(fu, rx, ry, rz, pa, py, pz, big, stage)
+    ghosts[...] = fine_ghosts(courant, g_o, g_c, spread, lhs)
+    fine_outer(0, fu, chg, edge_y, edge_z, ghosts, regs)
+    fine_update(courant, fu, chg, edge_y, edge_z)
+    fine_inner(fu, chg, edge_y, edge_z)
+    fine_outer(1, fu, chg, edge_y, edge_z, ghosts, regs)
+    fine_update(courant, fu, chg, edge_y, edge_z)
+    fine_results(fu, regs, pool, big, stage)
     for b in range(17):
         by_box[b] = stage[b * STAGE_ROWS : (b + 1) * STAGE_ROWS, :]
     for lane in range(64):
@@ -545,10 +596,7 @@
         ret.at[lanes_of_peer(me, BACK_ROWS), :], back.at[lanes_of_peer(me, BACK_ROWS), :], out_sem.at[0]
     )
     own.start()
-    for f in range(5):
-        for p in range(16):
-            fv[:, f, p * 256 : p * 256 + 256] = fu[f, :, (p + 1) * 256 : (p + 2) * 256]
-    store_fine = pltpu.make_async_copy(fv, fine_new, out_sem.at[1])
+    store_fine = pltpu.make_async_copy(fu, fine_new, out_sem.at[1])
     store_fine.start()
     for side in sides:
         side.wait()
@@ -631,24 +679,29 @@
     return jax.ShapeDtypeStruct(dims, F32)
 
 
-def step_call(box_lane, lane_box, coarse, keys, fine):
+def step_call(owner, corner, coarse, fine):
     peers = lax.axis_size("gx") * lax.axis_size("gz")
     count_y = lax.axis_size("gy")
     _, nx, ny, nz = coarse.shape
     dma = pltpu.SemaphoreType.DMA
-    tables = fine_tables()
 
     def vmem(*dims, dtype=F32):
         return pltpu.VMEM(dims, dtype)
 
     return pl.pallas_call(
         step_kernel,
-        out_shape=[shape(*coarse.shape), shape(*fine.shape), shape(64 * BACK_ROWS, 128), shape(8, 128)],
-        in_specs=[SMEM, SMEM, VMEM, VMEM, ANY] + [VMEM] * 6,
-        out_specs=[ANY, ANY, ANY, VMEM],
+        out_shape=[
+            shape(*coarse.shape),
+            shape(*fine.shape),
+            shape(64 * BACK_ROWS, 128),
+            shape(8, 128),
+            jax.ShapeDtypeStruct((8, nz), jnp.int32),
+        ],
+        in_specs=[SMEM, SMEM, VMEM, ANY],
+        out_specs=[ANY, ANY, ANY, VMEM, VMEM],
         scratch_shapes=[
             vmem(*fine.shape),
-            vmem(5, 16, 18 * 256),
+            vmem(*fine.shape),
             vmem(5, nx, ny, nz),
             vmem(5, nx, ny, nz),
             vmem(5, ny, nz),
@@ -667,17 +720,20 @@
             vmem(8, 128),
             vmem(16 * OUT_ROWS, 128),
             vmem(16 * OUT_ROWS, 128),
-            vmem(480, 128, dtype=BF16),
-            vmem(160, 2048),
-            vmem(160, 2048),
+            vmem(128, 512, dtype=BF16),
+            vmem(256, 128, dtype=BF16),
+            vmem(1440, 128, dtype=BF16),
+            vmem(480, 512),
             vmem(5, 16, 512),
-            vmem(5, 16, 2048),
-            vmem(5, 16, 2048),
-            vmem(2400, 256, dtype=BF16),
+            vmem(5, 16, 512),
+            vmem(240, 512),
+            vmem(3360, 256, dtype=BF16),
             vmem(17 * STAGE_ROWS, 128),
             vmem(64 * BACK_ROWS, 128),
             vmem(64, OUT_ROWS, 128),
             vmem(17, STAGE_ROWS, 128),
+            pltpu.SMEM((16,), jnp.int32),
+            pltpu.SMEM((64,), jnp.int32),
             dma((1,)),
             dma((3,)),
             *[dma((peers,))] * 6,
@@ -690,7 +746,7 @@
             collective_id=0, has_side_effects=True, vmem_limit_bytes=VMEM_LIMIT
         ),
         name="step",
-    )(box_lane, lane_box, coarse, keys, fine, *tables)
+    )(owner, corner, coarse, fine)
 
 
 def apply_call(base, keys, arr, gmax):
@@ -711,38 +767,12 @@
     )(base, keys, arr, gmax)
 
 
-def tables_of(slot_owner, box_corner, count_gz):
-    owners = slot_owner.reshape(-1)
-    slots = owners.shape[0]
-    index = jnp.arange(slots, dtype=jnp.int32)
-    rank = jnp.sum(
-        (owners[:, None] == owners[None, :]) & (index[None, :] < index[:, None]), axis=1, dtype=jnp.int32
+def local(coarse_old, fine_old, slot_owner, box_corner):
+    base, fine_new, back, gmax, keys = step_call(
+        slot_owner.reshape(-1), box_corner.T, coarse_old, fine_old.transpose(1, 0, 2)
     )
-    slot_lane = jnp.where(owners >= 0, owners * 2 + rank, -1)
-    lane_z = jnp.repeat(slot_lane, BOX)
-    spot = jnp.arange(slots * BOX, dtype=jnp.int32) % BOX
-    on = lane_z >= 0
-    inner = on & (spot >= SHIFT) & (spot < SHIFT + CORE)
-    outer = on & ((spot == SHIFT - 1) | (spot == SHIFT + CORE))
-    key_xy = jnp.where(inner, (spot - SHIFT) * 64 + lane_z, -1)
-    key_z = jnp.where(outer, jnp.where(spot < SHIFT, 0, 64) + lane_z, -1)
-    keys = jnp.stack([key_xy, key_z, lane_z] + [lane_z] * 5)
-    source = box_corner[:, 0] * count_gz + box_corner[:, 2] // slots
-    number = jnp.arange(source.shape[0], dtype=jnp.int32)
-    place = jnp.sum(
-        (source[:, None] == source[None, :]) & (number[None, :] < number[:, None]), axis=1, dtype=jnp.int32
-    )
-    box_lane = source * 2 + place
-    lanes = jnp.arange(64, dtype=jnp.int32)
-    lane_box = jnp.min(jnp.where(box_lane[None, :] == lanes[:, None], number[None, :], 16), axis=1)
-    return keys, box_lane, lane_box
-
-
-def local(coarse_old, fine_old, slot_owner, box_corner):
-    keys, box_lane, lane_box = tables_of(slot_owner, box_corner, lax.axis_size("gz"))
-    base, fine_new, back, gmax = step_call(box_lane, lane_box, coarse_old, keys, fine_old)
     coarse_new = apply_call(base, keys, back, gmax)
-    return (coarse_new, fine_new)
+    return (coarse_new, fine_new.transpose(1, 0, 2))
 
 
 def solution(mesh):

time: 105 us -> 90.7 us (0.86)
  local copies, waits for them, and re-layouts: 6.06 us -> 1.06 us
  other arithmetic: 4.69 us -> 0 us
  Pallas kernels: 93.4 us -> 88.9 us
    pallas_call x1, Pallas kernels: 87.8 us -> 83.3 us  [step_call(): pl.pallas_call(step_kernel, out_shape=[shape(*coarse.shape), shape(*fine....]
    unnamed x6 -> x3, local copies, waits for them, and re-layouts: 5.27 us -> 1.06 us
    add x2 -> x0, other arithmetic: 1.54 us -> none  [the longest x1 0.77 us: tables_of(): box_lane = source * 2 + place]
    reduce_sum x2 -> x0, other arithmetic: 1.09 us -> none  [the longest x1 0.91 us: tables_of(): jnp.sum((owners[:, None] == owners[None, :]) & (index[None, :] < index[:,...]
where the time goes in v3:
time: 90.7 us; the launch traced here: 90.6 us
  Pallas kernels  88.9 us (98%)
  local copies, waits for them, and re-layouts  1.06 us (1%)
    pallas_call x1, Pallas kernels, step_call(): pl.pallas_call(step_kernel, out_shape=[shape(*coarse.shape), shape(*fine....  83.3 us
    pallas_call x1, Pallas kernels, apply_call(): pl.pallas_call(apply_kernel, out_shape=shape(*base.shape), in_specs=[VMEM...  5.58 us

profile of v3, /device:TPU:4, one launch (start us, length us, event | category | flops | bytes accessed | tf_op | source)
XLA Modules:
  0.0 90.6 jit_solution(9736391056738153317)
XLA Ops:
  0.6 83.3 %step.1 = (f32[5,16,16,512]{3,2,1,0:T(8,128)}, f32[5,16,4096]{2,1,0:T(8,128)}, f32[2304,128]{1,0:T(8,128)}, f32[8,128]{1,0:T(8,128)}, s32[8,512]{1,0:T(8,128)}) custom-call(s32[32]{0:T(128)} %bitcast.7, s32[3,16]{1,0:T(4,128)} %bitcast.6, f32[5,16,16,512]{3,2,1,0:T(8,128)} %coarse.1, f32[5,16,4096]{2,1,0:T(8,128)} %bitcast.5), custom_call_target="tpu_custom_call" | custom-call | tf_op jit(solution)/shard_map/step/pallas_call | solution.py:691
  84.0 0.0 copy-start
  84.0 5.6 %reflux_apply.1 = f32[5,16,16,512]{3,2,1,0:T(8,128)} custom-call(f32[5,16,16,512]{3,2,1,0:T(8,128)} %get-tuple-element.7.base, s32[8,512]{1,0:T(8,128)} %get-tuple-element.8.keys, f32[2304,128]{1,0:T(8,128)} %get-tuple-element.9.arr, f32[8,128]{1,0:T(8,128)} %get-tuple-element.10.gmax), custom_call_target="tpu_custom_call" | custom-call | tf_op jit(solution)/shard_map/reflux_apply/pallas_call | solution.py:754
  89.5 0.0 copy-done
  89.6 1.1 %copy.7 = f32[16,5,4096]{2,0,1:T(8,128)} copy(f32[16,5,4096]{2,0,1:T(8,128)S(1)} %bitcast.4) | data formatting | bytes 2621440
Async XLA Ops:
  84.0 5.6 %copy-start = (f32[5,16,4096]{2,1,0:T(8,128)S(1)}, f32[5,16,4096]{2,1,0:T(8,128)}, u32[]{:S(2)}) copy-start(f32[5,16,4096]{2,1,0:T(8,128)} %get-tuple-element.11) | copy-start | bytes 3932164

commit v4 on v3

--- a/solution.py
+++ b/solution.py
@@ -10,8 +10,10 @@
 SHIFT = 4
 HEAT_RATIO = 1.4
 COURANT_NUMBER = 0.15
-OUT_ROWS = 16
-BACK_ROWS = 36
+OUT_ROWS = 15
+OUT_BLOCK = 32
+BACK_ROWS = 35
+BACK_BLOCK = 72
 STAGE_ROWS = 40
 MESH = pl.DeviceIdType.MESH
 F32 = jnp.float32
@@ -103,11 +105,15 @@
     )
 
 
-def lanes_of_peer(peer, rows):
-    return pl.ds(pl.multiple_of(peer * 2 * rows, 8), 2 * rows)
-
-
-def start_patches(pay, arr, rows, send, recv):
+def rows_of_lanes(part, block, rows, line):
+    return pl.ds(part % 4 * 8 * block + part // 4 * rows + line, 8, stride=block)
+
+
+def block_of(peer, block, rows):
+    return pl.ds(pl.multiple_of(peer * block, 8), rows)
+
+
+def start_patches(pay, arr, block, rows, send, recv):
     iy = lax.axis_index("gy")
     me = lax.axis_index("gx") * lax.axis_size("gz") + lax.axis_index("gz")
 
@@ -115,7 +121,7 @@
         x, z = plane_peer(s, 1)
         peer = x * lax.axis_size("gz") + z
         return remote(
-            pay.at[lanes_of_peer(peer, rows), :], arr.at[lanes_of_peer(me, rows), :], send.at[s], recv.at[s], (x, iy, z)
+            pay.at[block_of(peer, block, rows), :], arr.at[block_of(me, block, rows), :], send.at[s], recv.at[s], (x, iy, z)
         )
 
     @pl.loop(1, lax.axis_size("gx") * lax.axis_size("gz"))
@@ -141,7 +147,7 @@
 
     def put(line, tile):
         for part in range(8):
-            pay[pl.ds(part * 8 * OUT_ROWS + line, 8, stride=OUT_ROWS), :] = tile[part * 8 : part * 8 + 8]
+            pay[rows_of_lanes(part, OUT_BLOCK, OUT_ROWS, line), :] = tile[part * 8 : part * 8 + 8]
 
     for f in range(5):
         pieces = []
@@ -293,61 +299,78 @@
     return jnp.where(cell == wanted, 0.125, 0.0).astype(BF16)
 
 
+def roll_tiles(x, shift):
+    return jnp.concatenate([pltpu.roll(x[:, at : at + 128], shift, 1) for at in range(0, x.shape[1], 128)], axis=1)
+
+
 def plane_lanes(p):
     return pl.ds(pl.multiple_of(p * 256, 256), 256)
 
 
-def fine_inner(fu, chg, edge_y, edge_z):
-    lane = lax.broadcasted_iota(jnp.int32, (8, 256), 1)
-    inner_y = jnp.where(lane >= 16, 1.0, 0.0)
+def fine_inner(fu, chg, pflux, pspeed):
+    lane = lax.broadcasted_iota(jnp.int32, (16, 512), 1)
+    inner_y = jnp.where(lane & 255 >= 16, 1.0, 0.0)
     inner_z = jnp.where(lane & 15 != 0, 1.0, 0.0)
-    tile = lax.broadcasted_iota(jnp.int32, (8, 128), 1)
-
-    @pl.loop(0, 2)
-    def _(half):
-        rows = pl.ds(pl.multiple_of(half * 8, 8), 8)
-
-        def load(p):
-            return [fu[f, rows, plane_lanes(p)] for f in range(5)]
-
-        def plane(p, carry):
-            u, velocity, pressure, sound, lower = carry
-            prims = (velocity, pressure, sound)
-            after = load(jnp.minimum(p + 1, BOX - 1))
-            next_prims = speeds(after)
-            flux, speed = dirflux(u, prims, 0)
-            next_flux, next_speed = dirflux(after, next_prims, 0)
-            more = jnp.where(p < BOX - 1, 1.0, 0.0)
-            upper = [piece * more for piece in face(u, flux, speed, after, next_flux, next_speed)]
-            change = [a - b for a, b in zip(upper, lower)]
-            for d, shift, keep in ((1, 16, inner_y), (2, 1, inner_z)):
-                flux, speed = dirflux(u, prims, d)
-                ru = [pltpu.roll(piece, shift, 1) for piece in u]
-                rf = [ru[1 + d]] + [pltpu.roll(piece, shift, 1) for piece in flux[1:]]
-                low = face(ru, rf, pltpu.roll(speed, shift, 1), u, flux, speed)
-                low = [piece * keep for piece in low]
-                change = [c + (pltpu.roll(b, 256 - shift, 1) - b) for c, b in zip(change, low)]
-            seat = lax.rem(p, 8)
-            at = pl.multiple_of(p // 8 * 128, 128)
-            here_y = tile >> 4 == seat
-            here_z = tile & 15 == p
-            for f in range(5):
-                chg[f, rows, plane_lanes(p)] = change[f]
-                for side, shift in ((0, seat * 16), (1, lax.rem(seat * 16 + 16, 128))):
-                    moved = pltpu.roll(u[f][:, side * 128 : side * 128 + 128], shift, 1)
-                    place = pl.ds(side * 256 + at, 128)
-                    edge_y[f, rows, place] = jnp.where(here_y, moved, edge_y[f, rows, place])
-                for side, shift in ((0, p), (1, lax.rem(p + 113, 128))):
-                    for t in range(2):
-                        moved = pltpu.roll(u[f][:, t * 128 : t * 128 + 128], shift, 1)
-                        place = slice(side * 256 + t * 128, side * 256 + t * 128 + 128)
-                        edge_z[f, rows, place] = jnp.where(here_z, moved, edge_z[f, rows, place])
-            return after, next_prims[0], next_prims[1], next_prims[2], upper
-
-        first = load(0)
-        prims = speeds(first)
-        nothing = [jnp.zeros((8, 256), F32)] * 5
-        lax.fori_loop(0, BOX, plane, (first, prims[0], prims[1], prims[2], nothing))
+    for f in range(5):
+        pflux[f, :, 0:256] = jnp.zeros((16, 256), F32)
+    pspeed[:, 0:256] = jnp.zeros((16, 256), F32)
+
+    def pair(t, _):
+        first = t * 2
+        before = jnp.maximum(first - 1, 0)
+        both = pl.ds(pl.multiple_of(t * 512, 512), 512)
+        u = [fu[f, :, both] for f in range(5)]
+        prims = speeds(u)
+        flux, speed = dirflux(u, prims, 0)
+        lu = [jnp.concatenate([fu[f, :, plane_lanes(before)], u[f][:, :256]], axis=1) for f in range(5)]
+        lf = [jnp.concatenate([pflux[f, :, 0:256], flux[f][:, :256]], axis=1) for f in range(5)]
+        ls = jnp.concatenate([pspeed[:, 0:256], speed[:, :256]], axis=1)
+        lower = face(lu, lf, ls, u, flux, speed)
+        one = [jnp.where(t > 0, piece[:, :256], 0.0) for piece in lower]
+        two = [piece[:, 256:] for piece in lower]
+        for f in range(5):
+            pflux[f, :, 0:256] = flux[f][:, 256:]
+        pspeed[:, 0:256] = speed[:, 256:]
+        change = [jnp.concatenate([b - a, -b], axis=1) for a, b in zip(one, two)]
+        for d, shift, keep in ((1, 16, inner_y), (2, 1, inner_z)):
+
+            def turn(x, amount):
+                return pltpu.roll(x, amount % 512, 1) if d == 1 else roll_tiles(x, amount % 128)
+
+            flux, speed = dirflux(u, prims, d)
+            ru = [turn(piece, shift) for piece in u]
+            rf, rs = dirflux(ru, speeds(ru), d)
+            low = face(ru, rf, rs, u, flux, speed)
+            low = [piece * keep for piece in low]
+            change = [c + (turn(b, -shift) - b) for c, b in zip(change, low)]
+        for f in range(5):
+            chg[f, :, both] = change[f]
+            chg[f, :, plane_lanes(before)] = chg[f, :, plane_lanes(before)] + one[f]
+        return 0
+
+    lax.fori_loop(0, BOX // 2, pair, 0)
+
+
+def fine_edges(fu, edge_y, edge_z):
+    tile = lax.broadcasted_iota(jnp.int32, (16, 128), 1)
+
+    @pl.loop(0, 5)
+    def _(f):
+        for side in range(2):
+            for block in range(2):
+                cells = None
+                for seat in range(8):
+                    at = (block * 8 + seat) * 256 + side * 128
+                    moved = pltpu.roll(fu[f, :, at : at + 128], (seat + side) * 16 % 128, 1)
+                    cells = moved if cells is None else jnp.where(tile >> 4 == seat, moved, cells)
+                edge_y[f, :, side * 256 + block * 128 : side * 256 + block * 128 + 128] = cells
+            for block in range(2):
+                cells = None
+                for p in range(BOX):
+                    at = p * 256 + block * 128
+                    moved = pltpu.roll(fu[f, :, at : at + 128], (p + side * 113) % 128, 1)
+                    cells = moved if cells is None else jnp.where(tile & 15 == p, moved, cells)
+                edge_z[f, :, side * 256 + block * 128 : side * 256 + block * 128 + 128] = cells
 
 
 def fine_outer(sub, fu, chg, edge_y, edge_z, ghosts, regs):
@@ -383,7 +406,7 @@
     y_side = (tile < 16, tile >= 112)
     z_side = (tile & 15 == 0, tile & 15 == 15)
 
-    @pl.loop(0, BOX)
+    @pl.loop(0, BOX, unroll=16)
     def _(p):
         seat = lax.rem(p, 8)
         at = pl.multiple_of(p // 8 * 128, 128)
@@ -451,7 +474,7 @@
     rank = jnp.zeros(lane.shape, jnp.int32)
     for k in range(slots - 1):
         rank = rank + jnp.where((owners == owner[k]) & (slot > k), 1, 0)
-    seat = jnp.where(owners >= 0, owners * 2 + rank, -1)
+    seat = jnp.where(owners >= 0, rank * 32 + owners, -1)
     on = seat >= 0
     inner = on & (spot >= SHIFT) & (spot < SHIFT + CORE)
     keys[0:1, :] = jnp.where(inner, (spot - SHIFT) * 64 + seat, -1)[0:1]
@@ -468,7 +491,7 @@
         place = jnp.int32(0)
         for i in range(b):
             place = place + jnp.where(sources[i] == sources[b], 1, 0)
-        lanes.append(sources[b] * 2 + place)
+        lanes.append(jnp.minimum(place, 1) * 32 + sources[b])
         box_lane[b] = lanes[b]
 
     @pl.loop(0, 64)
@@ -507,11 +530,9 @@
     candidate_keys(owner, keys)
     exy[...] = onehot(keys[0:1, :], 512)
     pack(coarse, keys[1:2, :], exy, pay_o, cxy, cz, rxy)
-    for part in range(8):
-        pay_o[pl.ds(part * 8 * OUT_ROWS + 15, 8, stride=OUT_ROWS), :] = jnp.zeros((8, 128), F32)
     pl.semaphore_wait(barrier, peers - 1 + ny - 1)
-    old_patch = start_patches(pay_o, arr_o, OUT_ROWS, so, ro)
-    arr_o[lanes_of_peer(me, OUT_ROWS), :] = pay_o[lanes_of_peer(me, OUT_ROWS), :]
+    old_patch = start_patches(pay_o, arr_o, OUT_BLOCK, 30, so, ro)
+    arr_o[block_of(me, OUT_BLOCK, 30), :] = pay_o[block_of(me, OUT_BLOCK, 30), :]
 
     best = coarse_changes(coarse, keys[2:3, :], chgf, chgl, pflux, pspeed, hy, hz)
     load_fine.wait()
@@ -540,10 +561,10 @@
     for s in range(1, ny):
         best = jnp.maximum(best, tops[s])
     best = jnp.full((8, 128), jnp.max(best), F32)
-    for part in range(8):
-        pay_c[pl.ds(part * 8 * OUT_ROWS + 15, 8, stride=OUT_ROWS), :] = best
-    new_patch = start_patches(pay_c, arr_c, OUT_ROWS, sc, rc)
-    arr_c[lanes_of_peer(me, OUT_ROWS), :] = pay_c[lanes_of_peer(me, OUT_ROWS), :]
+    for part in range(4):
+        pay_c[pl.ds(part * 8 * OUT_BLOCK + 30, 8, stride=OUT_BLOCK), :] = best
+    new_patch = start_patches(pay_c, arr_c, OUT_BLOCK, 31, sc, rc)
+    arr_c[block_of(me, OUT_BLOCK, 31), :] = pay_c[block_of(me, OUT_BLOCK, 31), :]
     up_x, down_x = lax.rem(ix + 1, nx), lax.rem(ix + nx - 1, nx)
     up_y, down_y = lax.rem(iy + 1, ny), lax.rem(iy + ny - 1, ny)
     up_z, down_z = lax.rem(iz + 1, nz), lax.rem(iz + nz - 1, nz)
@@ -558,7 +579,8 @@
     for side in sides:
         side.start()
 
-    fine_inner(fu, chg, edge_y, edge_z)
+    fine_inner(fu, chg, pflux, pspeed)
+    fine_edges(fu, edge_y, edge_z)
     box_tables(corner, owner.shape[0], nz, box_lane, lane_box)
     spread[...] = spread_table()
     pool[...] = pool_table()
@@ -571,29 +593,32 @@
     def _(s):
         new_patch(s).wait()
 
-    for part in range(8):
-        best = jnp.maximum(best, arr_c[pl.ds(part * 8 * OUT_ROWS + 15, 8, stride=OUT_ROWS), :])
+    for part in range(4):
+        best = jnp.maximum(best, arr_c[pl.ds(part * 8 * OUT_BLOCK + 30, 8, stride=OUT_BLOCK), :])
     gmax[...] = best
     courant = COURANT_NUMBER / jnp.max(best)
     for arr, g in ((arr_o, g_o), (arr_c, g_c)):
         for lane in range(64):
-            by_lane[lane] = arr[lane * OUT_ROWS : (lane + 1) * OUT_ROWS, :]
+            at = lane % 32 * OUT_BLOCK + lane // 32 * OUT_ROWS
+            by_lane[lane] = arr[at : at + OUT_ROWS, :]
         for b in range(16):
             g[pl.ds(b, OUT_ROWS, stride=16), :] = by_lane[box_lane[b]]
     ghosts[...] = fine_ghosts(courant, g_o, g_c, spread, lhs)
     fine_outer(0, fu, chg, edge_y, edge_z, ghosts, regs)
     fine_update(courant, fu, chg, edge_y, edge_z)
-    fine_inner(fu, chg, edge_y, edge_z)
+    fine_inner(fu, chg, pflux, pspeed)
+    fine_edges(fu, edge_y, edge_z)
     fine_outer(1, fu, chg, edge_y, edge_z, ghosts, regs)
     fine_update(courant, fu, chg, edge_y, edge_z)
     fine_results(fu, regs, pool, big, stage)
     for b in range(17):
         by_box[b] = stage[b * STAGE_ROWS : (b + 1) * STAGE_ROWS, :]
     for lane in range(64):
-        ret[lane * BACK_ROWS : (lane + 1) * BACK_ROWS, :] = by_box[lane_box[lane]][:BACK_ROWS]
-    back_patch = start_patches(ret, back, BACK_ROWS, sr, rr)
+        at = lane % 32 * BACK_BLOCK + lane // 32 * BACK_ROWS
+        ret[at : at + BACK_ROWS, :] = by_box[lane_box[lane]][:BACK_ROWS]
+    back_patch = start_patches(ret, back, BACK_BLOCK, 70, sr, rr)
     own = pltpu.make_async_copy(
-        ret.at[lanes_of_peer(me, BACK_ROWS), :], back.at[lanes_of_peer(me, BACK_ROWS), :], out_sem.at[0]
+        ret.at[block_of(me, BACK_BLOCK, 70), :], back.at[block_of(me, BACK_BLOCK, 70), :], out_sem.at[0]
     )
     own.start()
     store_fine = pltpu.make_async_copy(fu, fine_new, out_sem.at[1])
@@ -612,15 +637,19 @@
         back_patch(s).wait()
 
 
-def apply_kernel(base, keys, arr, gmax, out, lxy, lz, dxy, dz):
-    nx, _, nz = base.shape[1:]
+def apply_kernel(base, keys, arr, gmax, fine, out, fine_out, body, boxes, lxy, lz, dxy, dz, sems):
+    nz = base.shape[3]
+    load = pltpu.make_async_copy(base, body, sems.at[5])
+    load.start()
+    load_fine = pltpu.make_async_copy(fine, boxes, sems.at[6])
+    load_fine.start()
     courant = COURANT_NUMBER / jnp.max(gmax[...])
     left = lax.broadcasted_iota(jnp.int32, (16, 128), 1) < 64
     left64 = lax.broadcasted_iota(jnp.int32, (64, 128), 1) < 64
 
     def lanes_of(line):
         return jnp.concatenate(
-            [arr[pl.ds(part * 8 * BACK_ROWS + line, 8, stride=BACK_ROWS), :] for part in range(8)], axis=0
+            [arr[rows_of_lanes(part, BACK_BLOCK, BACK_ROWS, line), :] for part in range(8)], axis=0
         )
 
     flat = [(f, i) for f in range(5) for i in range(6)]
@@ -646,28 +675,35 @@
         put_split(lz, f * 64, 320, jnp.where(left64, both[:64], both[64:]))
     dxy[...] = sum_split(dot_nn(lxy[...], onehot(keys[0:1, :], 512)))
     dz[...] = sum_split(dot_nn(lz[...], onehot(keys[1:2, :], 128)))
-
     spot = lax.broadcasted_iota(jnp.int32, (CORE, nz), 1) % BOX
     refined = jnp.broadcast_to(keys[2:3, :], (CORE, nz)) >= 0
     inside = refined & (spot >= SHIFT) & (spot < SHIFT + CORE)
     z_sign = courant * jnp.where(spot == SHIFT - 1, -1.0, jnp.where(spot == SHIFT + CORE, 1.0, 0.0))
     mid = slice(SHIFT, SHIFT + CORE)
-    for f in range(5):
-        for x in range(nx):
-            out[f, x] = base[f, x]
+    load_fine.wait()
+    store_fine = pltpu.make_async_copy(boxes, fine_out, sems.at[7])
+    store_fine.start()
+    load.wait()
+    stores = []
+    for f in range(5):
         for side, x, sign in ((0, SHIFT - 1, -1.0), (1, SHIFT + CORE, 1.0)):
             at = (f * 6 + 4) * 16 + side * 8
-            out[f, x, mid, :] = out[f, x, mid, :] + (sign * courant) * dxy[at : at + 8, :]
+            body[f, x, mid, :] = body[f, x, mid, :] + (sign * courant) * dxy[at : at + 8, :]
             at = (f * 6 + 5) * 16 + side * 8
+            y = x
             for i in range(CORE):
-                y = x
-                out[f, SHIFT + i, y : y + 1, :] = (
-                    out[f, SHIFT + i, y : y + 1, :] + (sign * courant) * dxy[at + i : at + i + 1, :]
+                body[f, SHIFT + i, y : y + 1, :] = (
+                    body[f, SHIFT + i, y : y + 1, :] + (sign * courant) * dxy[at + i : at + i + 1, :]
                 )
         for i in range(CORE):
-            fixed = out[f, SHIFT + i, mid, :] + z_sign * dz[f * 64 + i * 8 : f * 64 + i * 8 + 8, :]
+            fixed = body[f, SHIFT + i, mid, :] + z_sign * dz[f * 64 + i * 8 : f * 64 + i * 8 + 8, :]
             average = dxy[f * 96 + i * 8 : f * 96 + i * 8 + 8, :]
-            out[f, SHIFT + i, mid, :] = jnp.where(inside, average, fixed)
+            body[f, SHIFT + i, mid, :] = jnp.where(inside, average, fixed)
+        stores.append(pltpu.make_async_copy(body.at[f], out.at[f], sems.at[f]))
+        stores[f].start()
+    for store in stores:
+        store.wait()
+    store_fine.wait()
 
 
 VMEM = pl.BlockSpec(memory_space=pltpu.VMEM)
@@ -693,7 +729,7 @@
         out_shape=[
             shape(*coarse.shape),
             shape(*fine.shape),
-            shape(64 * BACK_ROWS, 128),
+            shape(32 * BACK_BLOCK, 128),
             shape(8, 128),
             jax.ShapeDtypeStruct((8, nz), jnp.int32),
         ],
@@ -710,7 +746,7 @@
             vmem(480, nz, dtype=BF16),
             vmem(960, nz, dtype=BF16),
             vmem(160, 512),
-            *[vmem(64 * OUT_ROWS, 128)] * 4,
+            *[vmem(32 * OUT_BLOCK, 128)] * 4,
             vmem(2, 5, nx, nz),
             vmem(2, 5, ny, 128),
             vmem(2, 5, ny, nz),
@@ -729,7 +765,7 @@
             vmem(240, 512),
             vmem(3360, 256, dtype=BF16),
             vmem(17 * STAGE_ROWS, 128),
-            vmem(64 * BACK_ROWS, 128),
+            vmem(32 * BACK_BLOCK, 128),
             vmem(64, OUT_ROWS, 128),
             vmem(17, STAGE_ROWS, 128),
             pltpu.SMEM((16,), jnp.int32),
@@ -749,29 +785,32 @@
     )(owner, corner, coarse, fine)
 
 
-def apply_call(base, keys, arr, gmax):
+def apply_call(base, keys, arr, gmax, fine):
     nz = base.shape[3]
     return pl.pallas_call(
         apply_kernel,
-        out_shape=shape(*base.shape),
-        in_specs=[VMEM] * 4,
-        out_specs=VMEM,
+        out_shape=[shape(*base.shape), shape(*fine.shape)],
+        in_specs=[ANY, VMEM, VMEM, VMEM, ANY],
+        out_specs=[ANY, ANY],
         scratch_shapes=[
+            pltpu.VMEM(base.shape, F32),
+            pltpu.VMEM(fine.shape, F32),
             pltpu.VMEM((1440, 512), BF16),
             pltpu.VMEM((960, 128), BF16),
             pltpu.VMEM((480, nz), F32),
             pltpu.VMEM((320, nz), F32),
+            pltpu.SemaphoreType.DMA((8,)),
         ],
         compiler_params=pltpu.CompilerParams(vmem_limit_bytes=VMEM_LIMIT),
         name="reflux_apply",
-    )(base, keys, arr, gmax)
+    )(base, keys, arr, gmax, fine)
 
 
 def local(coarse_old, fine_old, slot_owner, box_corner):
     base, fine_new, back, gmax, keys = step_call(
         slot_owner.reshape(-1), box_corner.T, coarse_old, fine_old.transpose(1, 0, 2)
     )
-    coarse_new = apply_call(base, keys, back, gmax)
+    coarse_new, fine_new = apply_call(base, keys, back, gmax, fine_new)
     return (coarse_new, fine_new.transpose(1, 0, 2))
 
 

time: 90.7 us -> 82.9 us (0.914)
  Pallas kernels: 88.9 us -> 82.1 us
  local copies, waits for them, and re-layouts: 1.06 us -> 0 us
    pallas_call x1, Pallas kernels: 83.3 us -> 76.7 us  [step_call(): pl.pallas_call(step_kernel, out_shape=[shape(*coarse.shape), shape(*fine....]
    unnamed x3 -> x0, local copies, waits for them, and re-layouts: 1.06 us -> none
where the time goes in v4:
time: 82.9 us; the launch traced here: 82.8 us
  Pallas kernels  82.1 us (99%)
    pallas_call x1, Pallas kernels, step_call(): pl.pallas_call(step_kernel, out_shape=[shape(*coarse.shape), shape(*fine....  76.7 us
    pallas_call x1, Pallas kernels, apply_call(): pl.pallas_call(apply_kernel, out_shape=[shape(*base.shape), shape(*fine.s...  5.4 us

profile of v4, /device:TPU:4, one launch (start us, length us, event | category | flops | bytes accessed | tf_op | source)
XLA Modules:
  0.0 82.8 jit_solution(863582593630204403)
XLA Ops:
  0.6 76.7 %step.1 = (f32[5,16,16,512]{3,2,1,0:T(8,128)}, f32[5,16,4096]{2,1,0:T(8,128)}, f32[2304,128]{1,0:T(8,128)}, f32[8,128]{1,0:T(8,128)}, s32[8,512]{1,0:T(8,128)}) custom-call(s32[32]{0:T(128)} %bitcast.6, s32[3,16]{1,0:T(4,128)} %bitcast.5, f32[5,16,16,512]{3,2,1,0:T(8,128)} %coarse.1, f32[5,16,4096]{2,1,0:T(8,128)} %bitcast.4), custom_call_target="tpu_custom_call" | custom-call | tf_op jit(solution)/shard_map/step/pallas_call | solution.py:727
  77.4 5.4 %reflux_apply.1 = (f32[5,16,16,512]{3,2,1,0:T(8,128)}, f32[5,16,4096]{2,1,0:T(8,128)}) custom-call(f32[5,16,16,512]{3,2,1,0:T(8,128)} %get-tuple-element.9.base, s32[8,512]{1,0:T(8,128)} %get-tuple-element.10.keys, f32[2304,128]{1,0:T(8,128)} %get-tuple-element.11.arr, f32[8,128]{1,0:T(8,128)} %get-tuple-element.12.gmax, f32[5,16,4096]{2,1,0:T(8,128)} %get-tuple-element.13.fine), custom_call_target="tpu_custom_call" | custom-call | tf_op jit(solution)/shard_map/reflux_apply/pallas_call | solution.py:790

commit v5 on v4

--- a/solution.py
+++ b/solution.py
@@ -382,7 +382,7 @@
                 inside = [fu[f, :, side * last : side * last + 256] for f in range(5)]
             else:
                 inside = [(edge_y, edge_z)[part - 1][f, :, lanes] for f in range(5)]
-            at = part * 160 + sub * 80
+            at = part * 80
             outside = [ghosts[at + f * 16 : at + f * 16 + 16, lanes] for f in range(5)]
             lower, upper = (outside, inside) if side == 0 else (inside, outside)
             fl, sl = dirflux(lower, speeds(lower), part)
@@ -424,14 +424,20 @@
                 fu[f, :, place] = fu[f, :, place] - courant * change
 
 
-def fine_ghosts(courant, g_o, g_c, spread, lhs):
+def fine_ghosts(cells, spread, lhs):
     for part in range(3):
         for f in range(5):
-            old = g_o[(f * 3 + part) * 16 : (f * 3 + part) * 16 + 16, :]
-            change = g_c[(f * 3 + part) * 16 : (f * 3 + part) * 16 + 16, :]
-            put_split(lhs, part * 160 + f * 16, 480, old)
-            put_split(lhs, part * 160 + 80 + f * 16, 480, 0.5 * (old + (old - courant * change)))
+            at = (f * 3 + part) * 16
+            put_split(lhs, part * 80 + f * 16, 240, cells[at : at + 16, :])
     return sum_split(dot_nn(lhs[...], spread[...]))
+
+
+def gather_boxes(arr, box_lane, by_lane, g):
+    for lane in range(64):
+        at = lane % 32 * OUT_BLOCK + lane // 32 * OUT_ROWS
+        by_lane[lane] = arr[at : at + OUT_ROWS, :]
+    for b in range(16):
+        g[pl.ds(b, OUT_ROWS, stride=16), :] = by_lane[box_lane[b]]
 
 
 def fine_results(fu, regs, pool, big, stage):
@@ -506,9 +512,9 @@
     owner, corner, coarse, fine,
     base, fine_new, back, gmax, keys,
     fu, chg, chgf, chgl, pflux, pspeed, exy, cxy, cz, rxy, pay_o, pay_c, arr_o, arr_c,
-    hy, hz, gx, gy, gz, tops, mine, g_o, g_c, spread, pool, lhs, ghosts, edge_y, edge_z, regs, big, stage,
+    hy, hz, gx, gy, gz, tops, mine, tops_all, mine_all, g_o, g_c, spread, pool, lhs, ghosts, edge_y, edge_z, regs, big, stage,
     ret, by_lane, by_box, box_lane, lane_box,
-    in_sem, out_sem, so, ro, sc, rc, sr, rr, hs, hr, ts, tr,
+    in_sem, out_sem, so, ro, sc, rc, sr, rr, us, ur, hs, hr, ts, tr,
 ):
     ix, iy, iz = (lax.axis_index(a) for a in ("gx", "gy", "gz"))
     nx, ny, nz = (lax.axis_size(a) for a in ("gx", "gy", "gz"))
@@ -560,11 +566,18 @@
     best = mine[...]
     for s in range(1, ny):
         best = jnp.maximum(best, tops[s])
-    best = jnp.full((8, 128), jnp.max(best), F32)
-    for part in range(4):
-        pay_c[pl.ds(part * 8 * OUT_BLOCK + 30, 8, stride=OUT_BLOCK), :] = best
-    new_patch = start_patches(pay_c, arr_c, OUT_BLOCK, 31, sc, rc)
-    arr_c[block_of(me, OUT_BLOCK, 31), :] = pay_c[block_of(me, OUT_BLOCK, 31), :]
+    mine_all[...] = jnp.full((1, 128), jnp.max(best), F32)
+
+    def plane_top(s):
+        x, z = plane_peer(s, 1)
+        return remote(mine_all, tops_all.at[s], us.at[s], ur.at[s], (x, iy, z))
+
+    @pl.loop(1, peers)
+    def _(s):
+        plane_top(s).start()
+
+    new_patch = start_patches(pay_c, arr_c, OUT_BLOCK, 30, sc, rc)
+    arr_c[block_of(me, OUT_BLOCK, 30), :] = pay_c[block_of(me, OUT_BLOCK, 30), :]
     up_x, down_x = lax.rem(ix + 1, nx), lax.rem(ix + nx - 1, nx)
     up_y, down_y = lax.rem(iy + 1, ny), lax.rem(iy + ny - 1, ny)
     up_z, down_z = lax.rem(iz + 1, nz), lax.rem(iz + nz - 1, nz)
@@ -589,25 +602,31 @@
     def _(s):
         old_patch(s).wait()
 
+    gather_boxes(arr_o, box_lane, by_lane, g_o)
+    ghosts[...] = fine_ghosts(g_o, spread, lhs)
+    fine_outer(0, fu, chg, edge_y, edge_z, ghosts, regs)
+
     @pl.loop(1, peers)
     def _(s):
-        new_patch(s).wait()
-
-    for part in range(4):
-        best = jnp.maximum(best, arr_c[pl.ds(part * 8 * OUT_BLOCK + 30, 8, stride=OUT_BLOCK), :])
-    gmax[...] = best
-    courant = COURANT_NUMBER / jnp.max(best)
-    for arr, g in ((arr_o, g_o), (arr_c, g_c)):
-        for lane in range(64):
-            at = lane % 32 * OUT_BLOCK + lane // 32 * OUT_ROWS
-            by_lane[lane] = arr[at : at + OUT_ROWS, :]
-        for b in range(16):
-            g[pl.ds(b, OUT_ROWS, stride=16), :] = by_lane[box_lane[b]]
-    ghosts[...] = fine_ghosts(courant, g_o, g_c, spread, lhs)
-    fine_outer(0, fu, chg, edge_y, edge_z, ghosts, regs)
+        plane_top(s).wait()
+
+    best = mine_all[...]
+    for s in range(1, peers):
+        best = jnp.maximum(best, tops_all[s])
+    fastest = jnp.max(best)
+    gmax[...] = jnp.full((8, 128), fastest, F32)
+    courant = COURANT_NUMBER / fastest
     fine_update(courant, fu, chg, edge_y, edge_z)
     fine_inner(fu, chg, pflux, pspeed)
     fine_edges(fu, edge_y, edge_z)
+
+    @pl.loop(1, peers)
+    def _(s):
+        new_patch(s).wait()
+
+    gather_boxes(arr_c, box_lane, by_lane, g_c)
+    g_c[...] = 0.5 * (g_o[...] + (g_o[...] - courant * g_c[...]))
+    ghosts[...] = fine_ghosts(g_c, spread, lhs)
     fine_outer(1, fu, chg, edge_y, edge_z, ghosts, regs)
     fine_update(courant, fu, chg, edge_y, edge_z)
     fine_results(fu, regs, pool, big, stage)
@@ -754,12 +773,14 @@
             vmem(2, 5, ny, 128),
             vmem(count_y, 8, 128),
             vmem(8, 128),
+            vmem(peers, 1, 128),
+            vmem(1, 128),
             vmem(16 * OUT_ROWS, 128),
             vmem(16 * OUT_ROWS, 128),
             vmem(128, 512, dtype=BF16),
             vmem(256, 128, dtype=BF16),
-            vmem(1440, 128, dtype=BF16),
-            vmem(480, 512),
+            vmem(720, 128, dtype=BF16),
+            vmem(240, 512),
             vmem(5, 16, 512),
             vmem(5, 16, 512),
             vmem(240, 512),
@@ -772,7 +793,7 @@
             pltpu.SMEM((64,), jnp.int32),
             dma((1,)),
             dma((3,)),
-            *[dma((peers,))] * 6,
+            *[dma((peers,))] * 8,
             dma((6,)),
             dma((6,)),
             dma((count_y,)),

time: 82.9 us -> 78.4 us (0.946)
  Pallas kernels: 82.1 us -> 77.6 us
    pallas_call x1, Pallas kernels: 76.7 us -> 72.2 us  [step_call(): pl.pallas_call(step_kernel, out_shape=[shape(*coarse.shape), shape(*fine....]
where the time goes in v5:
time: 78.4 us; the launch traced here: 78.2 us
  Pallas kernels  77.6 us (99%)
    pallas_call x1, Pallas kernels, step_call(): pl.pallas_call(step_kernel, out_shape=[shape(*coarse.shape), shape(*fine....  72.2 us
    pallas_call x1, Pallas kernels, apply_call(): pl.pallas_call(apply_kernel, out_shape=[shape(*base.shape), shape(*fine.s...  5.4 us

profile of v5, /device:TPU:4, one launch (start us, length us, event | category | flops | bytes accessed | tf_op | source)
XLA Modules:
  0.0 78.2 jit_solution(10525346308165596043)
XLA Ops:
  0.6 72.2 %step.1 = (f32[5,16,16,512]{3,2,1,0:T(8,128)}, f32[5,16,4096]{2,1,0:T(8,128)}, f32[2304,128]{1,0:T(8,128)}, f32[8,128]{1,0:T(8,128)}, s32[8,512]{1,0:T(8,128)}) custom-call(s32[32]{0:T(128)} %bitcast.6, s32[3,16]{1,0:T(4,128)} %bitcast.5, f32[5,16,16,512]{3,2,1,0:T(8,128)} %coarse.1, f32[5,16,4096]{2,1,0:T(8,128)} %bitcast.4), custom_call_target="tpu_custom_call" | custom-call | tf_op jit(solution)/shard_map/step/pallas_call | solution.py:746
  72.8 5.4 %reflux_apply.1 = (f32[5,16,16,512]{3,2,1,0:T(8,128)}, f32[5,16,4096]{2,1,0:T(8,128)}) custom-call(f32[5,16,16,512]{3,2,1,0:T(8,128)} %get-tuple-element.9.base, s32[8,512]{1,0:T(8,128)} %get-tuple-element.10.keys, f32[2304,128]{1,0:T(8,128)} %get-tuple-element.11.arr, f32[8,128]{1,0:T(8,128)} %get-tuple-element.12.gmax, f32[5,16,4096]{2,1,0:T(8,128)} %get-tuple-element.13.fine), custom_call_target="tpu_custom_call" | custom-call | tf_op jit(solution)/shard_map/reflux_apply/pallas_call | solution.py:811

commit v6 on v5

--- a/solution.py
+++ b/solution.py
@@ -600,7 +600,7 @@
 
     @pl.loop(1, peers)
     def _(s):
-        old_patch(s).wait()
+        old_patch(s).wait_recv()
 
     gather_boxes(arr_o, box_lane, by_lane, g_o)
     ghosts[...] = fine_ghosts(g_o, spread, lhs)
@@ -608,7 +608,7 @@
 
     @pl.loop(1, peers)
     def _(s):
-        plane_top(s).wait()
+        plane_top(s).wait_recv()
 
     best = mine_all[...]
     for s in range(1, peers):
@@ -622,10 +622,11 @@
 
     @pl.loop(1, peers)
     def _(s):
-        new_patch(s).wait()
+        new_patch(s).wait_recv()
 
     gather_boxes(arr_c, box_lane, by_lane, g_c)
-    g_c[...] = 0.5 * (g_o[...] + (g_o[...] - courant * g_c[...]))
+    used = slice(0, 16 * OUT_ROWS)
+    g_c[used, :] = 0.5 * (g_o[used, :] + (g_o[used, :] - courant * g_c[used, :]))
     ghosts[...] = fine_ghosts(g_c, spread, lhs)
     fine_outer(1, fu, chg, edge_y, edge_z, ghosts, regs)
     fine_update(courant, fu, chg, edge_y, edge_z)
@@ -653,6 +654,9 @@
 
     @pl.loop(1, peers)
     def _(s):
+        old_patch(s).wait_send()
+        plane_top(s).wait_send()
+        new_patch(s).wait_send()
         back_patch(s).wait()
 
 
@@ -748,7 +752,7 @@
         out_shape=[
             shape(*coarse.shape),
             shape(*fine.shape),
-            shape(32 * BACK_BLOCK, 128),
+            shape(33 * BACK_BLOCK, 128),
             shape(8, 128),
             jax.ShapeDtypeStruct((8, nz), jnp.int32),
         ],
@@ -765,7 +769,7 @@
             vmem(480, nz, dtype=BF16),
             vmem(960, nz, dtype=BF16),
             vmem(160, 512),
-            *[vmem(32 * OUT_BLOCK, 128)] * 4,
+            *[vmem(33 * OUT_BLOCK, 128)] * 4,
             vmem(2, 5, nx, nz),
             vmem(2, 5, ny, 128),
             vmem(2, 5, ny, nz),
@@ -775,8 +779,8 @@
             vmem(8, 128),
             vmem(peers, 1, 128),
             vmem(1, 128),
-            vmem(16 * OUT_ROWS, 128),
-            vmem(16 * OUT_ROWS, 128),
+            vmem(16 * OUT_ROWS + 16, 128),
+            vmem(16 * OUT_ROWS + 16, 128),
             vmem(128, 512, dtype=BF16),
             vmem(256, 128, dtype=BF16),
             vmem(720, 128, dtype=BF16),

time: 78.4 us -> 78.4 us (level)
  no operation moved by 1% of the time
where the time goes in v6:
time: 78.4 us; the launch traced here: 78.3 us
  Pallas kernels  77.6 us (99%)
    pallas_call x1, Pallas kernels, step_call(): pl.pallas_call(step_kernel, out_shape=[shape(*coarse.shape), shape(*fine....  72.2 us
    pallas_call x1, Pallas kernels, apply_call(): pl.pallas_call(apply_kernel, out_shape=[shape(*base.shape), shape(*fine.s...  5.41 us

profile of v6, /device:TPU:4, one launch (start us, length us, event | category | flops | bytes accessed | tf_op | source)
XLA Modules:
  0.0 78.3 jit_solution(9537877935840147953)
XLA Ops:
  0.6 72.2 %step.1 = (f32[5,16,16,512]{3,2,1,0:T(8,128)}, f32[5,16,4096]{2,1,0:T(8,128)}, f32[2376,128]{1,0:T(8,128)}, f32[8,128]{1,0:T(8,128)}, s32[8,512]{1,0:T(8,128)}) custom-call(s32[32]{0:T(128)} %bitcast.6, s32[3,16]{1,0:T(4,128)} %bitcast.5, f32[5,16,16,512]{3,2,1,0:T(8,128)} %coarse.1, f32[5,16,4096]{2,1,0:T(8,128)} %bitcast.4), custom_call_target="tpu_custom_call" | custom-call | tf_op jit(solution)/shard_map/step/pallas_call | solution.py:750
  72.8 5.4 %reflux_apply.1 = (f32[5,16,16,512]{3,2,1,0:T(8,128)}, f32[5,16,4096]{2,1,0:T(8,128)}) custom-call(f32[5,16,16,512]{3,2,1,0:T(8,128)} %get-tuple-element.9.base, s32[8,512]{1,0:T(8,128)} %get-tuple-element.10.keys, f32[2376,128]{1,0:T(8,128)} %get-tuple-element.11.arr, f32[8,128]{1,0:T(8,128)} %get-tuple-element.12.gmax, f32[5,16,4096]{2,1,0:T(8,128)} %get-tuple-element.13.fine), custom_call_target="tpu_custom_call" | custom-call | tf_op jit(solution)/shard_map/reflux_apply/pallas_call | solution.py:815
